TPU v7x, 32 devices: a whole 2x2x4 slice. The times are simulated.
32 devices in a mesh: dp: 16 (over z, y, core), tensor: 2 (over x).
Axes of the slice: x: 2, y: 2, z: 4, core: 2. Of those that a mesh axis runs over, the one named last changes fastest.
Arguments:
- hidden: bfloat16 [16384, 768], P(('dp', 'tensor')), may hold values from -6 to 6
- segments: int32 [16, 1024], P('dp'), may hold values from 0 to 3, as said below
- norm_gain: float32 [768], replicated, may hold values from 0.5 to 1.5
- proj_gate: bfloat16 [768, 1536], P('dp', 'tensor'), may hold values from -0.21875 to 0.21875
- proj_value: bfloat16 [768, 1536], P('dp', 'tensor'), may hold values from -0.21875 to 0.21875
- proj_bc: bfloat16 [768, 256], P(('dp', 'tensor')), may hold values from -0.21875 to 0.21875
- proj_step: bfloat16 [768, 24], P('dp', 'tensor'), may hold values from -0.21875 to 0.21875
- conv_value: float32 [4, 1536], P(None, 'tensor'), may hold values from -3 to 3
- conv_bc: float32 [4, 256], replicated, may hold values from -3 to 3
- conv_value_bias: float32 [1536], P('tensor'), may hold values from -3 to 3
- conv_bc_bias: float32 [256], replicated, may hold values from -3 to 3
- step_bias: float32 [24], P('tensor'), may hold values from -5 to -1
- decay_log: float32 [24], P('tensor'), may hold values from -3 to 1
- skip_gain: float32 [24], P('tensor'), may hold values from 0 to 2
- gate_gain: float32 [1536], P('tensor'), may hold values from 0.5 to 1.5
- out_weight: bfloat16 [768, 1536], P('dp', 'tensor'), may hold values from -0.15625 to 0.15625
- cotangent: bfloat16 [16384, 768], P(('dp', 'tensor')), may hold values from -6 to 6
Outputs:
- mixed: bfloat16 [16384, 768], P(('dp', 'tensor'))
- grad_hidden: float32 [16384, 768], P(('dp', 'tensor'))
- grad_norm_gain: float32 [768], replicated
- grad_proj_gate: float32 [768, 1536], P('dp', 'tensor')
- grad_proj_value: float32 [768, 1536], P('dp', 'tensor')
- grad_proj_bc: float32 [768, 256], P(('dp', 'tensor'))
- grad_proj_step: float32 [768, 24], P('dp', 'tensor')
- grad_conv_value: float32 [4, 1536], P(None, 'tensor')
- grad_conv_bc: float32 [4, 256], replicated
- grad_conv_value_bias: float32 [1536], P('tensor')
- grad_conv_bc_bias: float32 [256], replicated
- grad_step_bias: float32 [24], P('tensor')
- grad_decay_log: float32 [24], P('tensor')
- grad_skip_gain: float32 [24], P('tensor')
- grad_gate_gain: float32 [1536], P('tensor')
- grad_out_weight: float32 [768, 1536], P('dp', 'tensor')
Inputs may be any that keep to these rules, and one draw needn't show every extreme that they name: `segments`: within each packed sequence the numbers start at 0 and rise by one at each document start, so every sequence holds four documents, and one of them holds both token 511 and token 512.
All inputs are finite; a program needn't handle non-finite values.
Results may differ from a plain program's by a relative error of at most 0.0087.
Values may be sent and summed in bfloat16 or wider, within the bound.
A program may use at most 192 MiB of HBM per device.

v0:
```python
import jax
import jax.numpy as jnp
from jax import lax
from jax.sharding import PartitionSpec as P

D = 768
GROUP = 256
DI = 1536


EPS = 1e-05
HIGH = lax.Precision.HIGHEST


def conv_mix(stream, weight, offset, seg_row):
    width = weight.shape[0]
    length = stream.shape[0]
    padded = jnp.concatenate([jnp.zeros((width - 1, stream.shape[1]), stream.dtype), stream], 0)
    seg_pad = jnp.concatenate([jnp.full((width - 1,), -1, jnp.int32), seg_row], 0)
    summed = offset[None, :] + jnp.zeros_like(stream)
    for shift_by in range(width):
        first_row = width - 1 - shift_by
        window = padded[first_row : first_row + length]
        same_doc = (seg_pad[first_row : first_row + length] == seg_row).astype(stream.dtype)
        summed = summed + weight[width - 1 - shift_by][None, :] * window * same_doc[:, None]
    return summed


def block_scan_state(values, b_rows, c_rows, step_rows, seg_row, decay_rate):
    length, head_count, head_size = values.shape
    state_width = b_rows.shape[1]
    blocks = length // GROUP
    seg_blocks = seg_row.reshape(blocks, GROUP)
    prev_segs = jnp.concatenate([jnp.full((1,), -1, jnp.int32), seg_blocks[:-1, GROUP - 1]], 0)
    causal = jnp.arange(GROUP)[:, None] >= jnp.arange(GROUP)[None, :]

    def scan_step(carried, block_item):
        x_block, b_block, c_block, dt_block, seg_block, prev_seg = block_item
        cum_rate = jnp.cumsum(dt_block * decay_rate[None, :], axis=0)
        keep_mask = causal & (seg_block[:, None] == seg_block[None, :])
        exponent = jnp.where(
            keep_mask[None], cum_rate.T[:, :, None] - cum_rate.T[:, None, :], -jnp.inf
        )
        decay_in = jnp.exp(exponent)
        scores = jnp.dot(c_block, b_block.T, precision=HIGH)
        mixing = scores[None] * decay_in
        x_scaled = x_block * dt_block[:, :, None]
        y_inner = jnp.einsum("hts,shp->thp", mixing, x_scaled, precision=HIGH)
        carry_ok = (seg_block == prev_seg).astype(values.dtype)
        y_state = jnp.einsum("tn,hnp->thp", c_block, carried, precision=HIGH)
        y_state = y_state * (jnp.exp(cum_rate) * carry_ok[:, None])[:, :, None]
        block_total = cum_rate[GROUP - 1]
        tail_decay = (
            jnp.exp(block_total[None, :] - cum_rate)
            * (seg_block == seg_block[GROUP - 1]).astype(values.dtype)[:, None]
        )
        keep_state = jnp.exp(block_total) * (seg_block[GROUP - 1] == prev_seg).astype(values.dtype)
        new_state = carried * keep_state[:, None, None] + jnp.einsum(
            "sn,shp->hnp", b_block, x_scaled * tail_decay[:, :, None], precision=HIGH
        )
        return (new_state, y_inner + y_state)

    start_state = jnp.zeros((head_count, state_width, head_size), values.dtype)
    block_inputs = (
        values.reshape(blocks, GROUP, head_count, head_size),
        b_rows.reshape(blocks, GROUP, state_width),
        c_rows.reshape(blocks, GROUP, state_width),
        step_rows.reshape(blocks, GROUP, head_count),
        seg_blocks,
        prev_segs,
    )
    final_state, outputs = lax.scan(jax.checkpoint(scan_step), start_state, block_inputs)
    return (outputs.reshape(length, head_count, head_size), final_state)


def mixer(
    pre_gate,
    pre_value,
    pre_bc,
    pre_step,
    conv_value,
    conv_bc,
    conv_value_bias,
    conv_bc_bias,
    step_bias,
    decay_log,
    skip_gain,
    seg_row,
):
    length, inner_width = pre_value.shape
    head_count = pre_step.shape[1]
    head_size = inner_width // head_count
    state_width = pre_bc.shape[1] // 2
    stream = jnp.concatenate([pre_value, pre_bc], 1)
    taps = jnp.concatenate([conv_value, conv_bc], 1)
    offset = jnp.concatenate([conv_value_bias, conv_bc_bias], 0)
    activated = jax.nn.silu(conv_mix(stream, taps, offset, seg_row))
    values = activated[:, :inner_width].reshape(length, head_count, head_size)
    b_rows = activated[:, inner_width : inner_width + state_width]
    c_rows = activated[:, inner_width + state_width :]
    step_rows = jax.nn.softplus(pre_step + step_bias[None, :])
    decay_rate = -jnp.exp(decay_log)
    scanned, _ = block_scan_state(values, b_rows, c_rows, step_rows, seg_row, decay_rate)
    ssm_out = scanned + skip_gain[None, :, None] * values
    return ssm_out.reshape(length, inner_width) * jax.nn.silu(pre_gate)


def contract_rows(left, right):
    return lax.dot_general(
        left, right, (((0,), (0,)), ((), ())), preferred_element_type=jnp.float32
    )


def contract_cols(left, right):
    return lax.dot_general(
        left, right, (((1,), (1,)), ((), ())), preferred_element_type=jnp.float32
    )


def local(
    hidden,
    segments,
    norm_gain,
    proj_gate,
    proj_value,
    proj_bc,
    proj_step,
    conv_value,
    conv_bc,
    conv_value_bias,
    conv_bc_bias,
    step_bias,
    decay_log,
    skip_gain,
    gate_gain,
    out_weight,
    cotangent,
):
    seq_count, length = segments.shape
    own_index = lax.axis_index("tensor")
    tensor_count = lax.axis_size("tensor")
    residual = hidden.astype(jnp.float32)
    inv_rms = lax.rsqrt(jnp.mean(residual * residual, -1, keepdims=True) + EPS)
    normed = (residual * inv_rms * norm_gain[None, :]).astype(jnp.bfloat16)
    fwd_dp = (
        lax.all_gather(proj_gate, "dp", axis=0, tiled=True),
        lax.all_gather(proj_value, "dp", axis=0, tiled=True),
        lax.all_gather(proj_step, "dp", axis=0, tiled=True),
        lax.all_gather(out_weight, "dp", axis=0, tiled=True),
    )
    bc_full = lax.all_gather(proj_bc, ("dp", "tensor"), axis=0, tiled=True)
    rows_all = lax.all_gather(normed, "tensor", axis=0, tiled=True)
    gate_full, value_full, step_full, outw_full = fwd_dp
    pre_gate = jnp.dot(rows_all, gate_full, preferred_element_type=jnp.float32)
    pre_value = jnp.dot(rows_all, value_full, preferred_element_type=jnp.float32)
    pre_bc = jnp.dot(rows_all, bc_full, preferred_element_type=jnp.float32)
    pre_step = jnp.dot(rows_all, step_full, preferred_element_type=jnp.float32)

    def local_mixer(
        gate_in,
        value_in,
        bc_in,
        step_in,
        cv_taps,
        cbc_taps,
        cv_offset,
        cbc_offset,
        step_offset,
        decay_in,
        skip_in,
    ):
        mapped = jax.vmap(mixer, in_axes=(0, 0, 0, 0, None, None, None, None, None, None, None, 0))
        result = mapped(
            gate_in.reshape(seq_count, length, -1),
            value_in.reshape(seq_count, length, -1),
            bc_in.reshape(seq_count, length, -1),
            step_in.reshape(seq_count, length, -1),
            cv_taps,
            cbc_taps,
            cv_offset,
            cbc_offset,
            step_offset,
            decay_in,
            skip_in,
            segments,
        )
        return result.reshape(seq_count * length, -1)

    gated, pull_back = jax.vjp(
        local_mixer,
        pre_gate,
        pre_value,
        pre_bc,
        pre_step,
        conv_value,
        conv_bc,
        conv_value_bias,
        conv_bc_bias,
        step_bias,
        decay_log,
        skip_gain,
    )
    squares = lax.psum(jnp.sum(gated * gated, -1), "tensor")
    inv_gate = lax.rsqrt(squares / DI + EPS)[:, None]
    scaled = gated * inv_gate
    branch_in = (scaled * gate_gain[None, :]).astype(jnp.bfloat16)
    branch = lax.psum_scatter(
        contract_cols(branch_in, outw_full), "tensor", scatter_dimension=0, tiled=True
    )
    mixed_out = (residual + branch).astype(jnp.bfloat16)
    back_dp = (
        lax.all_gather(proj_gate, "dp", axis=0, tiled=True),
        lax.all_gather(proj_value, "dp", axis=0, tiled=True),
        lax.all_gather(proj_step, "dp", axis=0, tiled=True),
        lax.all_gather(out_weight, "dp", axis=0, tiled=True),
    )
    gate_back_w, value_back_w, step_back_w, outw_back = back_dp
    cot_all = lax.all_gather(cotangent, "tensor", axis=0, tiled=True)
    grad_out_w = contract_rows(cot_all, branch_in)
    grad_branch = jnp.dot(cot_all, outw_back, preferred_element_type=jnp.float32)
    grad_gate_gain = jnp.sum(grad_branch * scaled, 0)
    weighted = grad_branch * gate_gain[None, :]
    cross_sum = lax.psum(jnp.sum(weighted * gated, -1), "tensor")
    grad_gated = inv_gate * weighted - gated * inv_gate**3 * (cross_sum / DI)[:, None]
    (
        grad_pg,
        grad_pv,
        grad_pbc,
        grad_ps,
        grad_cv,
        grad_cbc,
        grad_cvb,
        grad_cbcb,
        grad_sb,
        grad_dl,
        grad_sk,
    ) = pull_back(grad_gated)
    low_gate = grad_pg.astype(jnp.bfloat16)
    low_value = grad_pv.astype(jnp.bfloat16)
    low_step = grad_ps.astype(jnp.bfloat16)
    grad_rows = (
        contract_cols(low_gate, gate_back_w)
        + contract_cols(low_value, value_back_w)
        + contract_cols(low_step, step_back_w)
    )
    grad_rows_own, grad_bc_own = (
        lax.psum_scatter(grad_rows, "tensor", scatter_dimension=0, tiled=True),
        lax.psum_scatter(grad_pbc, "tensor", scatter_dimension=0, tiled=True),
    )
    low_bc = grad_bc_own.astype(jnp.bfloat16)
    grad_normed = grad_rows_own + contract_cols(low_bc, bc_full)
    proj_parts = (
        contract_rows(rows_all, low_gate),
        contract_rows(rows_all, low_value),
        contract_rows(rows_all, low_step),
        grad_out_w,
    )

    def widen(values):
        span = values.shape[-1]
        widened = jnp.zeros(values.shape[:-1] + (span * tensor_count,), jnp.float32)
        return lax.dynamic_update_slice_in_dim(widened, values, own_index * span, values.ndim - 1)

    gw_gate, gw_value, gw_step, gw_out = (
        lax.psum_scatter(proj_parts[0], "dp", scatter_dimension=0, tiled=True),
        lax.psum_scatter(proj_parts[1], "dp", scatter_dimension=0, tiled=True),
        lax.psum_scatter(proj_parts[2], "dp", scatter_dimension=0, tiled=True),
        lax.psum_scatter(proj_parts[3], "dp", scatter_dimension=0, tiled=True),
    )
    gw_bc = contract_rows(normed, low_bc)
    gw_bc_own = lax.psum_scatter(gw_bc, ("dp", "tensor"), scatter_dimension=0, tiled=True)
    weighted_in = grad_normed * norm_gain[None, :]
    grad_norm_part = jnp.sum(grad_normed * residual * inv_rms, 0)
    grad_input = (
        cotangent.astype(jnp.float32)
        + inv_rms * weighted_in
        - residual * inv_rms**3 * jnp.sum(weighted_in * residual, -1, keepdims=True) / D
    )
    sum_norm, sum_cbc, sum_cbcb, wide_cv, wide_cvb, wide_sb, wide_dl, wide_sk, wide_gate = lax.psum(
        (
            grad_norm_part,
            grad_cbc,
            grad_cbcb,
            widen(grad_cv),
            widen(grad_cvb),
            widen(grad_sb),
            widen(grad_dl),
            widen(grad_sk),
            widen(grad_gate_gain),
        ),
        ("dp", "tensor"),
    )

    def narrow(values, span):
        return lax.dynamic_slice_in_dim(values, own_index * span, span, values.ndim - 1)

    sum_cv = narrow(wide_cv, conv_value.shape[-1])
    sum_cvb = narrow(wide_cvb, conv_value_bias.shape[-1])
    sum_sb = narrow(wide_sb, step_bias.shape[-1])
    sum_dl = narrow(wide_dl, decay_log.shape[-1])
    sum_sk = narrow(wide_sk, skip_gain.shape[-1])
    sum_gate = narrow(wide_gate, gate_gain.shape[-1])
    return (
        mixed_out,
        grad_input,
        sum_norm,
        gw_gate,
        gw_value,
        gw_bc_own,
        gw_step,
        sum_cv,
        sum_cbc,
        sum_cvb,
        sum_cbcb,
        sum_sb,
        sum_dl,
        sum_sk,
        sum_gate,
        gw_out,
    )


def solution(mesh):
    in_specs = (
        P(("dp", "tensor"), None),
        P("dp", None),
        P(),
        P("dp", "tensor"),
        P("dp", "tensor"),
        P(("dp", "tensor"), None),
        P("dp", "tensor"),
        P(None, "tensor"),
        P(),
        P("tensor"),
        P(),
        P("tensor"),
        P("tensor"),
        P("tensor"),
        P("tensor"),
        P("dp", "tensor"),
        P(("dp", "tensor"), None),
    )
    out_specs = (
        P(("dp", "tensor"), None),
        P(("dp", "tensor"), None),
        P(),
        P("dp", "tensor"),
        P("dp", "tensor"),
        P(("dp", "tensor"), None),
        P("dp", "tensor"),
        P(None, "tensor"),
        P(),
        P("tensor"),
        P(),
        P("tensor"),
        P("tensor"),
        P("tensor"),
        P("tensor"),
        P("dp", "tensor"),
    )
    return jax.shard_map(local, mesh=mesh, in_specs=in_specs, out_specs=out_specs, check_vma=False)
```

profile of v0, /device:TPU:0, one launch (start us, length us, event | category | flops | bytes accessed | tf_op | source)
XLA Modules:
  0.0 1109.0 jit_solution(12488063938804472735)
XLA Ops:
  18.7 23.3 %all-gather = bf16[16,48,12]{1,2,0:T(8,128)(2,1)S(1)} all-gather(bf16[1,48,12]{1,2,0:T(8,128)(2,1)S(1)} %bitcast.696), channel_id=1, replica_groups=mesh['dp'=16,'tensor'=2] {'dp'}, dimensions={0}, use_global_device_ids=true | all-gather | bytes 19584 | tf_op jit(solution)/shard_map/all_gather | solution.py:148
  42.1 67.4 %all_gather.28 = bf16[768,256]{1,0:T(8,128)(2,1)S(1)} all-gather(bf16[24,256]{1,0:T(8,128)(2,1)S(1)} %copy-done.76), channel_id=1, replica_groups=mesh['dp'=16,'tensor'=2] {'dp','tensor'}, dimensions={0}, use_global_device_ids=true | all-gather | bytes 405504 | tf_op jit(solution)/shard_map/all_gather | solution.py:151
  143.8 150.3 %while.41 = (s32[]{:T(128)}, f32[1,12,128,64]{2,3,1,0:T(8,128)S(1)}, f32[4,1,256,12,64]{2,0,4,3,1:T(4,128)}, f32[4,1,12,128,64]{3,4,2,1,0:T(8,128)}, f32[4,1,256...) while((s32[]{:T(128)}, ...), condition=%wide.region_4.5_spmd.clone, body=%wide.region_1.4_spmd.clone.sunk | while | flops 1312866304 | bytes 11175377 | solution.py:72
  163.5 17.9 %dynamic_update_slice.91 = f32[4,1,256,12,64]{2,0,4,3,1:T(4,128)} dynamic-update-slice(f32[4,1,256,12,64]{2,0,4,3,1:T(4,128)} %get-tuple-element.1261, f32[1,1,256,12,64]{2,0,4,3,1:T(1,128)S(1)} %copy.394, s32[]{:T(128)S(6)} %copy.425, s32[]{:T(128)} %constant.142.clone.1..sunk, s32[]{:T(128)} %constant.142.clone.1..sunk, s32[]{:T(128)} %constant.142.clone.1..sunk, s32[]{:T(128)} %constant.142.clone.1..sunk) | dynamic-update-slice | bytes 1572868 | tf_op jit(solution)/shard_map/jvp(vmap())/while/body/jit(dynamic_update_index_in_dim)/dynamic_update_slice | solution.py:72
  201.1 17.9 %dynamic_update_slice.91 = f32[4,1,256,12,64]{2,0,4,3,1:T(4,128)} dynamic-update-slice(f32[4,1,256,12,64]{2,0,4,3,1:T(4,128)} %get-tuple-element.1261, f32[1,1,256,12,64]{2,0,4,3,1:T(1,128)S(1)} %copy.394, s32[]{:T(128)S(6)} %copy.425, s32[]{:T(128)} %constant.142.clone.1..sunk, s32[]{:T(128)} %constant.142.clone.1..sunk, s32[]{:T(128)} %constant.142.clone.1..sunk, s32[]{:T(128)} %constant.142.clone.1..sunk) | dynamic-update-slice | bytes 1572868 | tf_op jit(solution)/shard_map/jvp(vmap())/while/body/jit(dynamic_update_index_in_dim)/dynamic_update_slice | solution.py:72
  238.7 17.9 %dynamic_update_slice.91 = f32[4,1,256,12,64]{2,0,4,3,1:T(4,128)} dynamic-update-slice(f32[4,1,256,12,64]{2,0,4,3,1:T(4,128)} %get-tuple-element.1261, f32[1,1,256,12,64]{2,0,4,3,1:T(1,128)S(1)} %copy.394, s32[]{:T(128)S(6)} %copy.425, s32[]{:T(128)} %constant.142.clone.1..sunk, s32[]{:T(128)} %constant.142.clone.1..sunk, s32[]{:T(128)} %constant.142.clone.1..sunk, s32[]{:T(128)} %constant.142.clone.1..sunk) | dynamic-update-slice | bytes 1572868 | tf_op jit(solution)/shard_map/jvp(vmap())/while/body/jit(dynamic_update_index_in_dim)/dynamic_update_slice | solution.py:72
  276.3 17.9 %dynamic_update_slice.91 = f32[4,1,256,12,64]{2,0,4,3,1:T(4,128)} dynamic-update-slice(f32[4,1,256,12,64]{2,0,4,3,1:T(4,128)} %get-tuple-element.1261, f32[1,1,256,12,64]{2,0,4,3,1:T(1,128)S(1)} %copy.394, s32[]{:T(128)S(6)} %copy.425, s32[]{:T(128)} %constant.142.clone.1..sunk, s32[]{:T(128)} %constant.142.clone.1..sunk, s32[]{:T(128)} %constant.142.clone.1..sunk, s32[]{:T(128)} %constant.142.clone.1..sunk) | dynamic-update-slice | bytes 1572868 | tf_op jit(solution)/shard_map/jvp(vmap())/while/body/jit(dynamic_update_index_in_dim)/dynamic_update_slice | solution.py:72
  298.5 8.1 multiply_reduce_fusion.11
  311.6 6.8 multiply_reduce_fusion.9
  337.7 262.9 %while.42 = (s32[]{:T(128)}, f32[12]{0:T(128)}, f32[1,12,128,64]{2,3,1,0:T(8,128)}, f32[4,1,256,12,64]{2,0,4,3,1:T(4,128)}, f32[4,1,256,128]{2,0,3,1:T(4,128)}, ...) while((s32[]{:T(128)}, f32[12]{0:T(128)}, ...), condition=%wide.region_24.25_spmd.clone, body=%wide.region_10.24_spmd.clone.sunk | while | flops 3033819136 | bytes 30547284 | solution.py:72
  393.1 17.9 %dynamic_update_slice.93 = f32[4,1,256,12,64]{2,0,4,3,1:T(4,128)} dynamic-update-slice(f32[4,1,256,12,64]{2,0,4,3,1:T(4,128)} %get-tuple-element.1310, f32[1,1,256,12,64]{2,0,4,3,1:T(1,128)S(1)} %copy.412, s32[]{:T(128)S(6)} %sub.268, s32[]{:T(128)} %constant.142.clone.1..sunk.1, s32[]{:T(128)} %constant.142.clone.1..sunk.1, s32[]{:T(128)} %constant.142.clone.1..sunk.1, s32[]{:T(128)} %constant.142.clone.1..sunk.1) | dynamic-update-slice | bytes 1572868 | tf_op jit(solution)/shard_map/transpose(jvp(vmap()))/while/body/jit(dynamic_update_index_in_dim)/dynamic_update_slice | solution.py:72
  456.2 17.9 %dynamic_update_slice.93 = f32[4,1,256,12,64]{2,0,4,3,1:T(4,128)} dynamic-update-slice(f32[4,1,256,12,64]{2,0,4,3,1:T(4,128)} %get-tuple-element.1310, f32[1,1,256,12,64]{2,0,4,3,1:T(1,128)S(1)} %copy.412, s32[]{:T(128)S(6)} %sub.268, s32[]{:T(128)} %constant.142.clone.1..sunk.1, s32[]{:T(128)} %constant.142.clone.1..sunk.1, s32[]{:T(128)} %constant.142.clone.1..sunk.1, s32[]{:T(128)} %constant.142.clone.1..sunk.1) | dynamic-update-slice | bytes 1572868 | tf_op jit(solution)/shard_map/transpose(jvp(vmap()))/while/body/jit(dynamic_update_index_in_dim)/dynamic_update_slice | solution.py:72
  519.4 17.9 %dynamic_update_slice.93 = f32[4,1,256,12,64]{2,0,4,3,1:T(4,128)} dynamic-update-slice(f32[4,1,256,12,64]{2,0,4,3,1:T(4,128)} %get-tuple-element.1310, f32[1,1,256,12,64]{2,0,4,3,1:T(1,128)S(1)} %copy.412, s32[]{:T(128)S(6)} %sub.268, s32[]{:T(128)} %constant.142.clone.1..sunk.1, s32[]{:T(128)} %constant.142.clone.1..sunk.1, s32[]{:T(128)} %constant.142.clone.1..sunk.1, s32[]{:T(128)} %constant.142.clone.1..sunk.1) | dynamic-update-slice | bytes 1572868 | tf_op jit(solution)/shard_map/transpose(jvp(vmap()))/while/body/jit(dynamic_update_index_in_dim)/dynamic_update_slice | solution.py:72
  582.5 17.9 %dynamic_update_slice.93 = f32[4,1,256,12,64]{2,0,4,3,1:T(4,128)} dynamic-update-slice(f32[4,1,256,12,64]{2,0,4,3,1:T(4,128)} %get-tuple-element.1310, f32[1,1,256,12,64]{2,0,4,3,1:T(1,128)S(1)} %copy.412, s32[]{:T(128)S(6)} %sub.268, s32[]{:T(128)} %constant.142.clone.1..sunk.1, s32[]{:T(128)} %constant.142.clone.1..sunk.1, s32[]{:T(128)} %constant.142.clone.1..sunk.1, s32[]{:T(128)} %constant.142.clone.1..sunk.1) | dynamic-update-slice | bytes 1572868 | tf_op jit(solution)/shard_map/transpose(jvp(vmap()))/while/body/jit(dynamic_update_index_in_dim)/dynamic_update_slice | solution.py:72
  608.1 7.1 add_bitcast_fusion.1
  617.1 7.0 multiply_reduce_fusion.8
  635.6 9.2 pad_add_fusion
  683.6 26.8 %reduce-scatter.25.cloned.1.call-done = f32[48,12]{1,0:T(8,128)} async-done(((f32[768,12]{1,0:T(8,128)}), f32[48,12]{1,0:T(8,128)}) %reduce-scatter.25.cloned.1.call-update) | async-done | bytes 2320
  711.8 43.2 %reduce-scatter.15.cloned.1.call-done = f32[512,768]{1,0:T(8,128)} async-done(((f32[1024,768]{1,0:T(8,128)}), f32[512,768]{1,0:T(8,128)}) %reduce-scatter.15.cloned.1.call-update) | async-done | bytes 1572880 | tf_op jit(solution)/shard_map/reduce_scatter | solution.py:247
  758.0 41.3 %all-reduce.14 = (f32[768]{0:T(1024)}, f32[4,1536]{1,0:T(4,128)S(1)}, f32[4,256]{1,0:T(4,128)}, f32[1536]{0:T(1024)S(1)}, f32[256]{0:T(256)}, /*index=5*/f32[24]...) all-reduce(f32[768]{0:T(1024)} %get-tuple-element.888, ...), channel_id=1, replica_groups=mesh['dp'=16,'tensor'=2] {'dp','tensor'}, use_global_device_ids=true, to_apply=%region_29.30 | all-reduce | flops 11336 | bytes 90688 | tf_op jit(solution)/shard_map/psum | solution.py:279
  806.4 96.5 %reduce-scatter.23.cloned.1.call-done = f32[24,256]{1,0:T(8,128)} async-done(((f32[768,256]{1,0:T(8,128)}), f32[24,256]{1,0:T(8,128)}) %reduce-scatter.23.cloned.1.call-update) | async-done | bytes 24592 | tf_op jit(solution)/shard_map/reduce_scatter | solution.py:271
  902.9 66.3 %reduce-scatter.27.cloned.1.call-done = f32[48,768]{1,0:T(8,128)} async-done(((f32[768,768]{1,0:T(8,128)}), f32[48,768]{1,0:T(8,128)}) %reduce-scatter.27.cloned.1.call-update) | async-done | bytes 147472
  969.2 66.7 %reduce-scatter.19.cloned.1.call-done = f32[48,768]{1,0:T(8,128)} async-done(((f32[768,768]{1,0:T(8,128)}), f32[48,768]{1,0:T(8,128)}) %reduce-scatter.19.cloned.1.call-update) | async-done | bytes 147472 | tf_op jit(solution)/shard_map/reduce_scatter | solution.py:265
  1036.0 66.3 %reduce-scatter.21.cloned.1.call-done = f32[48,768]{1,0:T(8,128)} async-done(((f32[768,768]{1,0:T(8,128)}), f32[48,768]{1,0:T(8,128)}) %reduce-scatter.21.cloned.1.call-update) | async-done | bytes 147472 | tf_op jit(solution)/shard_map/reduce_scatter | solution.py:266
  (799 shorter events, 391.0 us)
Async XLA Ops:
  7.2 102.9 %copy-start.82 = (f32[256]{0:T(256)S(1)}, f32[256]{0:T(256)}, u32[]{:S(2)}) copy-start(f32[256]{0:T(256)} %param.31) | copy-start | bytes 3076
  7.3 102.9 %copy-start.80 = (f32[768]{0:T(1024)S(1)}, f32[768]{0:T(1024)}, u32[]{:S(2)}) copy-start(f32[768]{0:T(1024)} %param.30) | copy-start | bytes 9220
  7.3 102.9 %copy-start.83 = (f32[12]{0:T(128)S(1)}, f32[12]{0:T(128)}, u32[]{:S(2)}) copy-start(f32[12]{0:T(128)} %param.32) | copy-start | bytes 148
  7.3 102.9 %all-gather.7.cloned.1.call-start = ((), (), s32[]{:S(2)}) async-start(), calls=%async_computation.8 | async-start | bytes 2359296 | tf_op jit(solution)/shard_map/all_gather | solution.py:152
  12.1 104.4 %all-gather.9.cloned.1.call-start = ((), (), s32[]{:S(2)}) async-start(), calls=%async_computation.9 | async-start | bytes 1253376 | tf_op jit(solution)/shard_map/all_gather | solution.py:147
  12.9 285.6 %all-gather.11.cloned.1.call-start = ((), (), s32[]{:S(2)}) async-start(), calls=%async_computation.10 | async-start | bytes 1253376 | tf_op jit(solution)/shard_map/all_gather | solution.py:146
  13.6 297.9 %all-gather.15.cloned.1.call-start = ((), (), s32[]{:S(2)}) async-start(), calls=%async_computation.13 | async-start | bytes 2359296 | tf_op jit(solution)/shard_map/all_gather | solution.py:218
  14.2 297.4 %all-gather.13.cloned.1.call-start = ((), (), s32[]{:S(2)}) async-start(), calls=%async_computation.11 | async-start | bytes 1253376 | tf_op jit(solution)/shard_map/all_gather | solution.py:149
  14.8 644.3 %reduce-scatter.17.cloned.1.call-start = ((), (), s32[]{:S(2)}) async-start(), calls=%async_computation.15 | async-start | bytes 1572864 | tf_op jit(solution)/shard_map/reduce_scatter | solution.py:248
  16.4 104.7 %copy-start.44 = (f32[1,1024]{1,0:T(1,128)}, f32[1,1024]{1,0:T(1,128)S(1)}, u32[]{:S(2)}) copy-start(f32[1,1024]{1,0:T(1,128)S(1)} %get-tuple-element.997) | copy-start | bytes 12292
  16.4 104.7 %copy-start.46 = (f32[1,1024]{1,0:T(1,128)}, f32[1,1024]{1,0:T(1,128)S(1)}, u32[]{:S(2)}) copy-start(f32[1,1024]{1,0:T(1,128)S(1)} %get-tuple-element.998) | copy-start | bytes 12292
  16.4 104.7 %copy-start.48 = (f32[1,1024]{1,0:T(1,128)}, f32[1,1024]{1,0:T(1,128)S(1)}, u32[]{:S(2)}) copy-start(f32[1,1024]{1,0:T(1,128)S(1)} %get-tuple-element.999) | copy-start | bytes 12292
  18.6 279.9 %copy-start.73 = (f32[768]{0:T(1024)}, f32[768]{0:T(1024)S(1)}, u32[]{:S(2)}) copy-start(f32[768]{0:T(1024)S(1)} %mul.927) | copy-start | bytes 9220
  18.6 102.4 %copy-start.55 = (f32[1,1024]{1,0:T(1,128)}, f32[1,1024]{1,0:T(1,128)S(1)}, u32[]{:S(2)}) copy-start(f32[1,1024]{1,0:T(1,128)S(1)} %get-tuple-element.989) | copy-start | bytes 12292
  18.7 102.4 %copy-start.57 = (f32[1,1024]{1,0:T(1,128)}, f32[1,1024]{1,0:T(1,128)S(1)}, u32[]{:S(2)}) copy-start(f32[1,1024]{1,0:T(1,128)S(1)} %get-tuple-element.990) | copy-start | bytes 12292
  18.7 102.4 %copy-start.59 = (f32[1,1024]{1,0:T(1,128)}, f32[1,1024]{1,0:T(1,128)S(1)}, u32[]{:S(2)}) copy-start(f32[1,1024]{1,0:T(1,128)S(1)} %get-tuple-element.991) | copy-start | bytes 12292
  633.4 77.0 %reduce-scatter.25.cloned.1.call-start = ((), (), s32[]{:S(2)}) async-start(), calls=%async_computation.19 | async-start | bytes 417792
  644.8 110.2 %reduce-scatter.15.cloned.1.call-start = ((), (), s32[]{:S(2)}) async-start(), calls=%async_computation.14 | async-start | bytes 4718592 | tf_op jit(solution)/shard_map/reduce_scatter | solution.py:247
  652.7 150.3 %reduce-scatter.13.cloned.1.call-start = ((), (), s32[]{:S(2)}) async-start(), calls=%async_computation.12 | async-start | bytes 4718592 | tf_op jit(solution)/shard_map/reduce_scatter | solution.py:207
  659.1 243.8 %reduce-scatter.23.cloned.1.call-start = ((), (), s32[]{:S(2)}) async-start(), calls=%async_computation.18 | async-start | bytes 811008 | tf_op jit(solution)/shard_map/reduce_scatter | solution.py:271
  662.5 306.7 %reduce-scatter.27.cloned.1.call-start = ((), (), s32[]{:S(2)}) async-start(), calls=%async_computation.20 | async-start | bytes 2506752
  671.1 364.9 %reduce-scatter.19.cloned.1.call-start = ((), (), s32[]{:S(2)}) async-start(), calls=%async_computation.16 | async-start | bytes 2506752 | tf_op jit(solution)/shard_map/reduce_scatter | solution.py:265
  674.1 428.2 %reduce-scatter.21.cloned.1.call-start = ((), (), s32[]{:S(2)}) async-start(), calls=%async_computation.17 | async-start | bytes 2506752 | tf_op jit(solution)/shard_map/reduce_scatter | solution.py:266
  679.2 123.8 %copy-start.25 = (bf16[512,768]{1,0:T(8,128)(2,1)S(1)}, bf16[512,768]{1,0:T(8,128)(2,1)}, u32[]{:S(2)}) copy-start(bf16[512,768]{1,0:T(8,128)(2,1)} %param.37) | copy-start | bytes 2359300
  (126 other events, 1249.4 us)
Sparse Core Ops, SparseCore 0:
  12.3 29.8 all-gather.6
  44.5 38.9 all-gather.8
  85.8 37.2 all-gather.10
  124.5 26.1 all-gather.14
  152.9 38.3 all-gather.12
  633.6 17.2 reduce-scatter.16
  654.7 55.6 reduce-scatter.24
  712.7 42.3 reduce-scatter.14
  757.4 44.5 reduce-scatter.12
  807.5 95.3 reduce-scatter.22
  907.2 61.9 reduce-scatter.26
  973.9 62.0 reduce-scatter.18
  1040.3 61.9 reduce-scatter.20
where the time goes:
time: 1120 us; the launch traced here: 1110 us
  waiting for transfers between devices  369 us (33%)
  local copies, waits for them, and re-layouts  300 us (27%)
  matrix products  157 us (14%)
  blocking collectives  142 us (13%)
  other arithmetic  101 us (9%)
  loops' own time  24.1 us (2%)
  between operations  14.9 us (1%)
    dynamic_update_slice x28, local copies, waits for them, and re-layouts, block_scan_state(): lax.scan(jax.checkpoint(scan_step), start_state, block_inputs)  174 us
    reduce_scatter x1, waiting for transfers between devices, local(): lax.psum_scatter(gw_bc, ('dp', 'tensor'), scatter_dimension=0, tiled=True)  96.5 us
    unnamed x15, waiting for transfers between devices  95.8 us
    all_gather x1, blocking collectives, local(): bc_full = lax.all_gather(proj_bc, ('dp', 'tensor'), axis=0, tiled=True)  67.4 us
    reduce_scatter x1, waiting for transfers between devices, local(): lax.psum_scatter(proj_parts[0], 'dp', scatter_dimension=0, tiled=True)  66.7 us
    reduce_scatter x1, waiting for transfers between devices, local(): lax.psum_scatter(proj_parts[1], 'dp', scatter_dimension=0, tiled=True)  66.3 us
    dot_general x12, matrix products, scan_step(): y_inner = jnp.einsum('hts,shp->thp', mixing, x_scaled, precision=HIGH)  52.9 us
    reduce_scatter x1, waiting for transfers between devices, local(): lax.psum_scatter(grad_rows, 'tensor', scatter_dimension=0, tiled=True)  43.2 us
  transfers between devices with their start and end apart: 13, of which 6 were waited for; matrix products, arithmetic and copies ran while one was open for 23% of the time, Pallas kernels for 0%

commit v1 on v0

--- a/solution.py
+++ b/solution.py
@@ -1,6 +1,8 @@
 import jax
 import jax.numpy as jnp
 from jax import lax
+from jax.experimental import pallas as pl
+from jax.experimental.pallas import tpu as pltpu
 from jax.sharding import PartitionSpec as P
 
 D = 768
@@ -117,6 +119,238 @@
     )
 
 
+VMEM_LIMIT = 56 * 2**20
+
+
+def flipped(index, pattern, bits):
+    result = index
+    for bit in bits:
+        if pattern & bit:
+            result = result + bit * (1 - 2 * lax.rem(index // bit, 2))
+    return result
+
+
+def greet(partners):
+    barrier = pltpu.get_barrier_semaphore()
+    for partner in partners:
+        pl.semaphore_signal(
+            barrier, inc=1, device_id=partner, device_id_type=pl.DeviceIdType.MESH
+        )
+    pl.semaphore_wait(barrier, len(partners))
+
+
+def gather_kernel(bits, own_ref, full_ref, held, send_sem, recv_sem, out_sem):
+    me = lax.axis_index("dp")
+    greet([{"dp": flipped(me, bit, bits)} for bit in bits])
+    held[me] = own_ref[...]
+    copies = {}
+
+    def forward(pattern, below):
+        chunk = flipped(me, pattern, bits)
+        for bit in reversed(bits):
+            if bit < below:
+                arrives = pattern ^ bit
+                copies[arrives] = pltpu.make_async_remote_copy(
+                    src_ref=held.at[chunk],
+                    dst_ref=held.at[chunk],
+                    send_sem=send_sem.at[arrives],
+                    recv_sem=recv_sem.at[arrives],
+                    device_id={"dp": flipped(me, bit, bits)},
+                    device_id_type=pl.DeviceIdType.MESH,
+                )
+                copies[arrives].start()
+
+    total = 2 * bits[-1]
+    forward(0, total)
+    for low in reversed(bits):
+        for pattern in range(low, total, 2 * low):
+            copies[pattern].wait_recv()
+            forward(pattern, low)
+    for copy in copies.values():
+        copy.wait_send()
+    out = pltpu.make_async_copy(held, full_ref, out_sem)
+    out.start()
+    out.wait()
+
+
+def gather_rows(own, count):
+    bits = [1 << power for power in range(count.bit_length() - 1)]
+    rows, columns = own.shape
+    full = pl.pallas_call(
+        lambda *refs: gather_kernel(bits, *refs),
+        out_shape=jax.ShapeDtypeStruct((count, rows, columns), own.dtype),
+        in_specs=[pl.BlockSpec(memory_space=pltpu.VMEM)],
+        out_specs=pl.BlockSpec(memory_space=pl.ANY),
+        scratch_shapes=[
+            pltpu.VMEM((count, rows, columns), own.dtype),
+            pltpu.SemaphoreType.DMA((count,)),
+            pltpu.SemaphoreType.DMA((count,)),
+            pltpu.SemaphoreType.DMA,
+        ],
+        compiler_params=pltpu.CompilerParams(
+            collective_id=0, has_side_effects=True, vmem_limit_bytes=VMEM_LIMIT
+        ),
+        name="gather_rows",
+    )(own)
+    return full.reshape(count * rows, columns)
+
+
+def scatter_kernel(
+    bits,
+    bc_from,
+    parts_ref,
+    small_ref,
+    sum_ref,
+    bc_ref,
+    small_out,
+    slots,
+    staged,
+    bc_sum,
+    bc_got,
+    small_sent,
+    small_got,
+    send_sem,
+    recv_sem,
+    bc_sem,
+    small_send,
+    small_recv,
+):
+    me = lax.axis_index("dp")
+    half = lax.axis_index("tensor")
+    other = 1 - half
+    partners = [{"dp": flipped(me, bit, bits)} for bit in bits] + [{"tensor": other}]
+    greet(partners)
+    total = 2 * bits[-1]
+    copies = {}
+
+    def lowest(pattern):
+        return pattern & -pattern
+
+    def send(pattern, source):
+        copies[pattern] = pltpu.make_async_remote_copy(
+            src_ref=source,
+            dst_ref=slots.at[pattern],
+            send_sem=send_sem.at[pattern],
+            recv_sem=recv_sem.at[pattern],
+            device_id={"dp": flipped(me, lowest(pattern), bits)},
+            device_id_type=pl.DeviceIdType.MESH,
+        )
+        copies[pattern].start()
+
+    def summed(pattern):
+        value = parts_ref[flipped(me, pattern, bits)].astype(jnp.float32)
+        for bit in bits:
+            if pattern == 0 or bit < lowest(pattern):
+                copies[pattern + bit].wait_recv()
+                value = value + slots[pattern + bit].astype(jnp.float32)
+        return value
+
+    odd = sorted(range(1, total, 2), key=lambda p: (lowest(p - 1) if p > 1 else total, p))
+    for pattern in odd:
+        send(pattern, parts_ref.at[flipped(me, pattern, bits)])
+
+    small_sent[0] = small_ref[...]
+    small_copies = []
+
+    def small_step(step):
+        copy = pltpu.make_async_remote_copy(
+            src_ref=small_sent.at[step],
+            dst_ref=small_got.at[step],
+            send_sem=small_send.at[step],
+            recv_sem=small_recv.at[step],
+            device_id=partners[step],
+            device_id_type=pl.DeviceIdType.MESH,
+        )
+        copy.start()
+        small_copies.append(copy)
+
+    small_step(0)
+    for step, bit in enumerate(bits[1:]):
+        for pattern in range(bit, total, 2 * bit):
+            staged[pattern] = summed(pattern).astype(staged.dtype)
+            send(pattern, staged.at[pattern])
+        small_copies[step].wait_recv()
+        small_sent[step + 1] = small_sent[step] + small_got[step]
+        small_step(step + 1)
+    value = summed(0)
+    sum_ref[...] = value
+    last = len(bits)
+    bc_sum[...] = value[:, bc_from : bc_from + bc_sum.shape[1]]
+    span = bc_ref.shape[0]
+    bc_copy = pltpu.make_async_remote_copy(
+        src_ref=bc_sum.at[pl.ds(pl.multiple_of(other * span, 8), span)],
+        dst_ref=bc_got,
+        send_sem=bc_sem.at[0],
+        recv_sem=bc_sem.at[1],
+        device_id={"tensor": other},
+        device_id_type=pl.DeviceIdType.MESH,
+    )
+    bc_copy.start()
+    small_copies[last - 1].wait_recv()
+    small_sent[last] = small_sent[last - 1] + small_got[last - 1]
+    small_step(last)
+    small_copies[last].wait_recv()
+    small_out[:8] = small_sent[last, :8]
+    small_out[8:] = small_sent[last, 8:] + small_got[last, 8:]
+    bc_copy.wait_recv()
+    bc_ref[...] = bc_sum[pl.ds(pl.multiple_of(half * span, 8), span)] + bc_got[...]
+    bc_copy.wait_send()
+    for copy in list(copies.values()) + small_copies:
+        copy.wait_send()
+
+
+def scatter_rows(parts, small, count, bc_from, bc_width):
+    bits = [1 << power for power in range(count.bit_length() - 1)]
+    rows, columns = parts.shape[0] // count, parts.shape[1]
+    steps = len(bits) + 1
+    vmem = pl.BlockSpec(memory_space=pltpu.VMEM)
+    return pl.pallas_call(
+        lambda *refs: scatter_kernel(bits, bc_from, *refs),
+        out_shape=(
+            jax.ShapeDtypeStruct((rows, columns), jnp.float32),
+            jax.ShapeDtypeStruct((rows // 2, bc_width), jnp.float32),
+            jax.ShapeDtypeStruct(small.shape, jnp.float32),
+        ),
+        in_specs=[vmem, vmem],
+        out_specs=(vmem, vmem, vmem),
+        scratch_shapes=[
+            pltpu.VMEM((count, rows, columns), parts.dtype),
+            pltpu.VMEM((count, rows, columns), parts.dtype),
+            pltpu.VMEM((rows, bc_width), jnp.float32),
+            pltpu.VMEM((rows // 2, bc_width), jnp.float32),
+            pltpu.VMEM((steps,) + small.shape, jnp.float32),
+            pltpu.VMEM((steps,) + small.shape, jnp.float32),
+            pltpu.SemaphoreType.DMA((count,)),
+            pltpu.SemaphoreType.DMA((count,)),
+            pltpu.SemaphoreType.DMA((2,)),
+            pltpu.SemaphoreType.DMA((steps,)),
+            pltpu.SemaphoreType.DMA((steps,)),
+        ],
+        compiler_params=pltpu.CompilerParams(
+            collective_id=1, has_side_effects=True, vmem_limit_bytes=VMEM_LIMIT
+        ),
+        name="scatter_rows",
+    )(parts.reshape(count, rows, columns), small)
+
+
+def swap(values):
+    return lax.ppermute(values, "tensor", [(0, 1), (1, 0)])
+
+
+def both_halves(own, index):
+    got = swap(own)
+    return jnp.where(
+        index == 0, jnp.concatenate([own, got], 0), jnp.concatenate([got, own], 0)
+    )
+
+
+def own_half(values, index):
+    span = values.shape[0] // 2
+    away = lax.dynamic_slice_in_dim(values, (1 - index) * span, span, 0)
+    kept = lax.dynamic_slice_in_dim(values, index * span, span, 0)
+    return kept + swap(away.astype(jnp.bfloat16)).astype(jnp.float32)
+
+
 def local(
     hidden,
     segments,
@@ -138,53 +372,42 @@
 ):
     seq_count, length = segments.shape
     own_index = lax.axis_index("tensor")
-    tensor_count = lax.axis_size("tensor")
+    count = lax.axis_size("dp")
+    rows = proj_gate.shape[0]
+    inner = proj_gate.shape[1]
+    bc_width = proj_bc.shape[1]
+    head_count = proj_step.shape[1]
+    step_pad = -head_count % 128
+    bc_from = 3 * inner
+    step_from = bc_from + bc_width
+    direct = rows % 16 == 0 and count & (count - 1) == 0
     residual = hidden.astype(jnp.float32)
     inv_rms = lax.rsqrt(jnp.mean(residual * residual, -1, keepdims=True) + EPS)
     normed = (residual * inv_rms * norm_gain[None, :]).astype(jnp.bfloat16)
-    fwd_dp = (
-        lax.all_gather(proj_gate, "dp", axis=0, tiled=True),
-        lax.all_gather(proj_value, "dp", axis=0, tiled=True),
-        lax.all_gather(proj_step, "dp", axis=0, tiled=True),
-        lax.all_gather(out_weight, "dp", axis=0, tiled=True),
-    )
-    bc_full = lax.all_gather(proj_bc, ("dp", "tensor"), axis=0, tiled=True)
-    rows_all = lax.all_gather(normed, "tensor", axis=0, tiled=True)
-    gate_full, value_full, step_full, outw_full = fwd_dp
+    bc_pair = both_halves(proj_bc, own_index)
+    own_weights = jnp.concatenate(
+        [proj_value, proj_gate, out_weight, bc_pair, jnp.pad(proj_step, ((0, 0), (0, step_pad)))], 1
+    )
+    rows_all = both_halves(normed, own_index)
+    cot_all = both_halves(cotangent, own_index)
+    if direct:
+        weights = gather_rows(own_weights, count)
+    else:
+        weights = lax.all_gather(own_weights, "dp", axis=0, tiled=True)
+    value_full = weights[:, :inner]
+    gate_full = weights[:, inner : 2 * inner]
+    outw_full = weights[:, 2 * inner : 3 * inner]
+    bc_full = weights[:, bc_from:step_from]
+    step_full = weights[:, step_from:]
     pre_gate = jnp.dot(rows_all, gate_full, preferred_element_type=jnp.float32)
     pre_value = jnp.dot(rows_all, value_full, preferred_element_type=jnp.float32)
     pre_bc = jnp.dot(rows_all, bc_full, preferred_element_type=jnp.float32)
-    pre_step = jnp.dot(rows_all, step_full, preferred_element_type=jnp.float32)
-
-    def local_mixer(
-        gate_in,
-        value_in,
-        bc_in,
-        step_in,
-        cv_taps,
-        cbc_taps,
-        cv_offset,
-        cbc_offset,
-        step_offset,
-        decay_in,
-        skip_in,
-    ):
-        mapped = jax.vmap(mixer, in_axes=(0, 0, 0, 0, None, None, None, None, None, None, None, 0))
-        result = mapped(
-            gate_in.reshape(seq_count, length, -1),
-            value_in.reshape(seq_count, length, -1),
-            bc_in.reshape(seq_count, length, -1),
-            step_in.reshape(seq_count, length, -1),
-            cv_taps,
-            cbc_taps,
-            cv_offset,
-            cbc_offset,
-            step_offset,
-            decay_in,
-            skip_in,
-            segments,
-        )
-        return result.reshape(seq_count * length, -1)
+    pre_step = jnp.dot(rows_all, step_full, preferred_element_type=jnp.float32)[:, :head_count]
+    grad_branch = jnp.dot(cot_all, outw_full, preferred_element_type=jnp.float32)
+    weighted = grad_branch * gate_gain[None, :]
+
+    def local_mixer(*inputs):
+        return mixer(*inputs, segments.reshape(-1))
 
     gated, pull_back = jax.vjp(
         local_mixer,
@@ -200,28 +423,16 @@
         decay_log,
         skip_gain,
     )
-    squares = lax.psum(jnp.sum(gated * gated, -1), "tensor")
-    inv_gate = lax.rsqrt(squares / DI + EPS)[:, None]
-    scaled = gated * inv_gate
-    branch_in = (scaled * gate_gain[None, :]).astype(jnp.bfloat16)
-    branch = lax.psum_scatter(
-        contract_cols(branch_in, outw_full), "tensor", scatter_dimension=0, tiled=True
-    )
+    sums = jnp.stack([jnp.sum(gated * gated, -1), jnp.sum(weighted * gated, -1)], 0)
+    sums = sums + swap(sums)
+    inv_gate = lax.rsqrt(sums[0] / DI + EPS)[:, None]
+    cross = (sums[1] / DI)[:, None]
+    branch_in = (gated * inv_gate * gate_gain[None, :]).astype(jnp.bfloat16)
+    branch = own_half(contract_cols(branch_in, outw_full), own_index)
     mixed_out = (residual + branch).astype(jnp.bfloat16)
-    back_dp = (
-        lax.all_gather(proj_gate, "dp", axis=0, tiled=True),
-        lax.all_gather(proj_value, "dp", axis=0, tiled=True),
-        lax.all_gather(proj_step, "dp", axis=0, tiled=True),
-        lax.all_gather(out_weight, "dp", axis=0, tiled=True),
-    )
-    gate_back_w, value_back_w, step_back_w, outw_back = back_dp
-    cot_all = lax.all_gather(cotangent, "tensor", axis=0, tiled=True)
     grad_out_w = contract_rows(cot_all, branch_in)
-    grad_branch = jnp.dot(cot_all, outw_back, preferred_element_type=jnp.float32)
-    grad_gate_gain = jnp.sum(grad_branch * scaled, 0)
-    weighted = grad_branch * gate_gain[None, :]
-    cross_sum = lax.psum(jnp.sum(weighted * gated, -1), "tensor")
-    grad_gated = inv_gate * weighted - gated * inv_gate**3 * (cross_sum / DI)[:, None]
+    grad_gate_gain = jnp.sum(grad_branch * gated * inv_gate, 0)
+    grad_gated = inv_gate * weighted - gated * inv_gate**3 * cross
     (
         grad_pg,
         grad_pv,
@@ -237,38 +448,12 @@
     ) = pull_back(grad_gated)
     low_gate = grad_pg.astype(jnp.bfloat16)
     low_value = grad_pv.astype(jnp.bfloat16)
-    low_step = grad_ps.astype(jnp.bfloat16)
-    grad_rows = (
-        contract_cols(low_gate, gate_back_w)
-        + contract_cols(low_value, value_back_w)
-        + contract_cols(low_step, step_back_w)
-    )
-    grad_rows_own, grad_bc_own = (
-        lax.psum_scatter(grad_rows, "tensor", scatter_dimension=0, tiled=True),
-        lax.psum_scatter(grad_pbc, "tensor", scatter_dimension=0, tiled=True),
-    )
-    low_bc = grad_bc_own.astype(jnp.bfloat16)
+    low_step = jnp.pad(grad_ps, ((0, 0), (0, step_pad))).astype(jnp.bfloat16)
+    grad_rows = contract_cols(low_gate, gate_full) + contract_cols(low_value, value_full)
+    grad_rows = grad_rows + contract_cols(low_step, step_full)
+    grad_rows_own = own_half(grad_rows, own_index)
+    low_bc = own_half(grad_pbc, own_index).astype(jnp.bfloat16)
     grad_normed = grad_rows_own + contract_cols(low_bc, bc_full)
-    proj_parts = (
-        contract_rows(rows_all, low_gate),
-        contract_rows(rows_all, low_value),
-        contract_rows(rows_all, low_step),
-        grad_out_w,
-    )
-
-    def widen(values):
-        span = values.shape[-1]
-        widened = jnp.zeros(values.shape[:-1] + (span * tensor_count,), jnp.float32)
-        return lax.dynamic_update_slice_in_dim(widened, values, own_index * span, values.ndim - 1)
-
-    gw_gate, gw_value, gw_step, gw_out = (
-        lax.psum_scatter(proj_parts[0], "dp", scatter_dimension=0, tiled=True),
-        lax.psum_scatter(proj_parts[1], "dp", scatter_dimension=0, tiled=True),
-        lax.psum_scatter(proj_parts[2], "dp", scatter_dimension=0, tiled=True),
-        lax.psum_scatter(proj_parts[3], "dp", scatter_dimension=0, tiled=True),
-    )
-    gw_bc = contract_rows(normed, low_bc)
-    gw_bc_own = lax.psum_scatter(gw_bc, ("dp", "tensor"), scatter_dimension=0, tiled=True)
     weighted_in = grad_normed * norm_gain[None, :]
     grad_norm_part = jnp.sum(grad_normed * residual * inv_rms, 0)
     grad_input = (
@@ -276,47 +461,63 @@
         + inv_rms * weighted_in
         - residual * inv_rms**3 * jnp.sum(weighted_in * residual, -1, keepdims=True) / D
     )
-    sum_norm, sum_cbc, sum_cbcb, wide_cv, wide_cvb, wide_sb, wide_dl, wide_sk, wide_gate = lax.psum(
-        (
-            grad_norm_part,
-            grad_cbc,
-            grad_cbcb,
-            widen(grad_cv),
-            widen(grad_cvb),
-            widen(grad_sb),
-            widen(grad_dl),
-            widen(grad_sk),
-            widen(grad_gate_gain),
-        ),
-        ("dp", "tensor"),
-    )
-
-    def narrow(values, span):
-        return lax.dynamic_slice_in_dim(values, own_index * span, span, values.ndim - 1)
-
-    sum_cv = narrow(wide_cv, conv_value.shape[-1])
-    sum_cvb = narrow(wide_cvb, conv_value_bias.shape[-1])
-    sum_sb = narrow(wide_sb, step_bias.shape[-1])
-    sum_dl = narrow(wide_dl, decay_log.shape[-1])
-    sum_sk = narrow(wide_sk, skip_gain.shape[-1])
-    sum_gate = narrow(wide_gate, gate_gain.shape[-1])
+    parts = jnp.concatenate(
+        [
+            contract_rows(rows_all, low_value),
+            contract_rows(rows_all, low_gate),
+            grad_out_w,
+            contract_rows(normed, low_bc),
+            contract_rows(rows_all, low_step),
+        ],
+        1,
+    )
+
+    def as_row(values):
+        flat = values.reshape(1, -1)
+        return jnp.pad(flat, ((0, 0), (0, inner - flat.shape[1])))
+
+    bc_rows = -(-4 * bc_width // inner)
+    small = jnp.concatenate(
+        [
+            grad_cv,
+            as_row(grad_cvb),
+            as_row(grad_gate_gain),
+            as_row(jnp.concatenate([grad_sb, grad_dl, grad_sk])),
+            as_row(grad_norm_part[:0]),
+            as_row(grad_norm_part),
+            as_row(grad_cbcb),
+            jnp.pad(grad_cbc.reshape(-1), (0, bc_rows * inner - 4 * bc_width)).reshape(bc_rows, inner),
+            jnp.zeros((6 - bc_rows, inner), jnp.float32),
+        ],
+        0,
+    )
+    if direct:
+        gw, gw_bc, small = scatter_rows(parts.astype(jnp.bfloat16), small, count, bc_from, bc_width)
+    else:
+        gw = lax.psum_scatter(parts, "dp", scatter_dimension=0, tiled=True)
+        gw_bc = lax.psum_scatter(
+            gw[:, bc_from:step_from], "tensor", scatter_dimension=0, tiled=True
+        )
+        small = lax.psum(small, "dp")
+        small = jnp.concatenate([small[:8], lax.psum(small[8:], "tensor")], 0)
+    heads = small[6]
     return (
         mixed_out,
         grad_input,
-        sum_norm,
-        gw_gate,
-        gw_value,
-        gw_bc_own,
-        gw_step,
-        sum_cv,
-        sum_cbc,
-        sum_cvb,
-        sum_cbcb,
-        sum_sb,
-        sum_dl,
-        sum_sk,
-        sum_gate,
-        gw_out,
+        small[8],
+        gw[:, inner : 2 * inner],
+        gw[:, :inner],
+        gw_bc,
+        gw[:, step_from : step_from + head_count],
+        small[:4],
+        small[10 : 10 + bc_rows].reshape(-1)[: 4 * bc_width].reshape(4, bc_width),
+        small[4],
+        small[9, :bc_width],
+        heads[:head_count],
+        heads[head_count : 2 * head_count],
+        heads[2 * head_count : 3 * head_count],
+        small[5],
+        gw[:, 2 * inner : 3 * inner],
     )
 
 

time: 1120 us -> 636 us (0.57)
  waiting for transfers between devices: 369 us -> 11.8 us
  blocking collectives: 142 us -> 0 us
  Pallas kernels: 0 us -> 93.4 us
  local copies, waits for them, and re-layouts: 300 us -> 275 us
  matrix products: 157 us -> 137 us
  other arithmetic: 101 us -> 85.9 us
  between operations: 14.9 us -> 1.81 us
  loops' own time: 24.1 us -> 12.5 us
    reduce_scatter x6 -> x0, waiting for transfers between devices: 273 us -> none  [the longest x1 96.5 us: local(): lax.psum_scatter(gw_bc, ('dp', 'tensor'), scatter_dimension=0, tiled=True)]
    unnamed x15 -> x0, waiting for transfers between devices: 95.8 us -> none
    pallas_call x0 -> x2, Pallas kernels: none -> 93.4 us  [the longest x1 56 us: scatter_rows(): pl.pallas_call(lambda *refs: scatter_kernel(bits, bc_from, *refs), out_sh...]
    all_gather x2 -> x0, blocking collectives: 90.6 us -> none  [the longest x1 67.4 us: local(): bc_full = lax.all_gather(proj_bc, ('dp', 'tensor'), axis=0, tiled=True)]
    psum x3 -> x0, blocking collectives: 51.1 us -> none  [the longest x1 41.3 us: local(): lax.psum((grad_norm_part, grad_cbc, grad_cbcb, widen(grad_cv), widen(grad...]
    dynamic_update_slice x28 -> x24, local copies, waits for them, and re-layouts: 174 us -> 155 us  [block_scan_state(): lax.scan(jax.checkpoint(scan_step), start_state, block_inputs)]
    ppermute x0 -> x7, waiting for transfers between devices: none -> 11.8 us  [swap(): return lax.ppermute(values, 'tensor', [(0, 1), (1, 0)])]
    another operation x2, loops' own time: 24.1 us -> 12.5 us  [block_scan_state(): lax.scan(jax.checkpoint(scan_step), start_state, block_inputs)]
  transfers between devices with their start and end apart: 13 -> 7, of which waited for: 6 -> 2; matrix products, arithmetic and copies ran while one was open for 23% -> 33% of each run, Pallas kernels for 0% -> 15%
where the time goes in v1:
time: 636 us; the launch traced here: 626 us
  local copies, waits for them, and re-layouts  275 us (43%)
  matrix products  137 us (22%)
  Pallas kernels  93.4 us (15%)
  other arithmetic  85.9 us (14%)
  loops' own time  12.5 us (2%)
  waiting for transfers between devices  11.8 us (2%)
  starting transfers between devices  8.33 us (1%)
    dynamic_update_slice x24, local copies, waits for them, and re-layouts, block_scan_state(): lax.scan(jax.checkpoint(scan_step), start_state, block_inputs)  155 us
    pallas_call x1, Pallas kernels, scatter_rows(): pl.pallas_call(lambda *refs: scatter_kernel(bits, bc_from, *refs), out_sh...  56 us
    dot_general x12, matrix products, scan_step(): y_inner = jnp.einsum('hts,shp->thp', mixing, x_scaled, precision=HIGH)  53.8 us
    pallas_call x1, Pallas kernels, gather_rows(): pl.pallas_call(lambda *refs: gather_kernel(bits, *refs), out_shape=jax.Sh...  37.4 us
    unnamed x153, local copies, waits for them, and re-layouts  34.6 us
    dynamic_slice x20, local copies, waits for them, and re-layouts, block_scan_state(): lax.scan(jax.checkpoint(scan_step), start_state, block_inputs)  20.7 us
    another operation x44, other arithmetic  19.5 us
    dot_general x12, matrix products, scan_step(): jnp.einsum('sn,shp->hnp', b_block, x_scaled * tail_decay[:, :, None], pre...  16.5 us
  transfers between devices with their start and end apart: 7, of which 2 were waited for; matrix products, arithmetic and copies ran while one was open for 33% of the time, Pallas kernels for 15%

profile of v1, /device:TPU:0, one launch (start us, length us, event | category | flops | bytes accessed | tf_op | source)
XLA Modules:
  0.0 625.6 jit_solution(15881057110312698957)
XLA Ops:
  21.3 37.4 %gather_rows.1 = bf16[16,48,2688]{2,1,0:T(8,128)(2,1)} custom-call(bf16[48,2688]{1,0:T(8,128)(2,1)} %copy-done.29), custom_call_target="tpu_custom_call" | custom-call | tf_op jit(solution)/shard_map/gather_rows/pallas_call | solution.py:179
  64.7 6.1 fusion.96
  89.7 136.4 %while.41 = (s32[]{:T(128)}, f32[12,128,64]{1,2,0:T(8,128)S(1)}, f32[4,256,12,64]{1,0,3,2:T(4,128)}, f32[4,12,128,64]{2,3,1,0:T(8,128)}, f32[4,256,12]{1,2,0:T(8...) while((s32[]{:T(128)}, f32[12,128,64]{1,2,0:T(8,128)S(1)}, ...), condition=%wide.region_4.5_spmd.clone, body=%wide.region_1.4_spmd.clone.sunk | while | flops 1312863232 | bytes 10986209 | solution.py:74
  97.0 4.8 fusion.230
  102.6 17.9 %dynamic_update_slice.66 = f32[4,256,12,64]{1,0,3,2:T(4,128)} dynamic-update-slice(f32[4,256,12,64]{1,0,3,2:T(4,128)} %get-tuple-element.1223, f32[1,256,12,64]{1,0,3,2:T(1,128)S(1)} %copy.290, s32[]{:T(128)} %get-tuple-element.1221, s32[]{:T(128)} %constant.140.clone.1..sunk, s32[]{:T(128)} %constant.140.clone.1..sunk, s32[]{:T(128)} %constant.140.clone.1..sunk) | dynamic-update-slice | bytes 1572868 | tf_op jit(solution)/shard_map/jvp()/while/body/jit(dynamic_update_index_in_dim)/dynamic_update_slice | solution.py:74
  131.0 4.8 fusion.230
  136.7 17.9 %dynamic_update_slice.66 = f32[4,256,12,64]{1,0,3,2:T(4,128)} dynamic-update-slice(f32[4,256,12,64]{1,0,3,2:T(4,128)} %get-tuple-element.1223, f32[1,256,12,64]{1,0,3,2:T(1,128)S(1)} %copy.290, s32[]{:T(128)} %get-tuple-element.1221, s32[]{:T(128)} %constant.140.clone.1..sunk, s32[]{:T(128)} %constant.140.clone.1..sunk, s32[]{:T(128)} %constant.140.clone.1..sunk) | dynamic-update-slice | bytes 1572868 | tf_op jit(solution)/shard_map/jvp()/while/body/jit(dynamic_update_index_in_dim)/dynamic_update_slice | solution.py:74
  165.1 4.8 fusion.230
  170.7 17.9 %dynamic_update_slice.66 = f32[4,256,12,64]{1,0,3,2:T(4,128)} dynamic-update-slice(f32[4,256,12,64]{1,0,3,2:T(4,128)} %get-tuple-element.1223, f32[1,256,12,64]{1,0,3,2:T(1,128)S(1)} %copy.290, s32[]{:T(128)} %get-tuple-element.1221, s32[]{:T(128)} %constant.140.clone.1..sunk, s32[]{:T(128)} %constant.140.clone.1..sunk, s32[]{:T(128)} %constant.140.clone.1..sunk) | dynamic-update-slice | bytes 1572868 | tf_op jit(solution)/shard_map/jvp()/while/body/jit(dynamic_update_index_in_dim)/dynamic_update_slice | solution.py:74
  199.2 4.8 fusion.230
  204.8 17.9 %dynamic_update_slice.66 = f32[4,256,12,64]{1,0,3,2:T(4,128)} dynamic-update-slice(f32[4,256,12,64]{1,0,3,2:T(4,128)} %get-tuple-element.1223, f32[1,256,12,64]{1,0,3,2:T(1,128)S(1)} %copy.290, s32[]{:T(128)} %get-tuple-element.1221, s32[]{:T(128)} %constant.140.clone.1..sunk, s32[]{:T(128)} %constant.140.clone.1..sunk, s32[]{:T(128)} %constant.140.clone.1..sunk) | dynamic-update-slice | bytes 1572868 | tf_op jit(solution)/shard_map/jvp()/while/body/jit(dynamic_update_index_in_dim)/dynamic_update_slice | solution.py:74
  234.1 6.7 %multiply_reduce_fusion.12 = (f32[1024]{0:T(1024)S(1)}, f32[1024]{0:T(1024)S(1)}, f32[1024,768]{0,1:T(8,128)}, f32[1024,768]{0,1:T(8,128)}) fusion(f32[768]{0:T(1024)S(1)} %copy-done.71, f32[1024,768]{0,1:T(8,128)S(1)} %fusion.118, f32[1024,768]{0,1:T(8,128)S(1)} %bitcast.381, f32[1024,1024]{0,1:T(8,128)S(1)} %copy-done.2, f32[768]{0:T(1024)S(1)} %mul.839, ...), kind=kOutput, calls=%fused_computation.178 | convolution fusion | flops 1224472576 | bytes 18497536 | tf_op jit(solution)/shard_map/dot_general | solution.py:406
  244.6 8.5 %multiply_reduce_fusion.9 = (f32[768]{0:T(1024)}, f32[1024,768]{0,1:T(8,128)S(1)}, bf16[1024,768]{0,1:T(8,128)(2,1)}, f32[768]{0:T(1024)}) fusion(f32[1024,1024]{0,1:T(8,128)} %copy-done.1, f32[1024,768]{0,1:T(8,128)} %copy-done.21, f32[1024]{0:T(1024)S(1)} %bitcast.443, f32[1024,768]{0,1:T(8,128)} %get-tuple-element.919, ...), kind=kLoop, calls=%fused_computation.171 | loop fusion | flops 19659264 | bytes 20471808 | tf_op jit(solution)/shard_map/transpose(jvp())/reduce_sum | solution.py:106
  261.0 217.9 %while.42 = (s32[]{:T(128)}, f32[12]{0:T(128)}, f32[12,128,64]{1,2,0:T(8,128)S(1)}, f32[4,256,12,64]{1,0,3,2:T(4,128)}, f32[4,256,128]{2,1,0:T(8,128)}, /*index=...) while((s32[]{:T(128)}, f32[12]{0:T(128)}, ...), condition=%wide.region_21.22_spmd.clone, body=%wide.region_7.21_spmd.clone.sunk | while | flops 3033812992 | bytes 31205752 | solution.py:74
  289.3 17.9 %dynamic_update_slice.69 = f32[4,256,12,64]{1,0,3,2:T(4,128)} dynamic-update-slice(f32[4,256,12,64]{1,0,3,2:T(4,128)} %get-tuple-element.1274, f32[1,256,12,64]{1,0,3,2:T(1,128)S(1)} %copy.305, s32[]{:T(128)S(6)} %sub.287, s32[]{:T(128)} %constant.140.clone.1..sunk.1, s32[]{:T(128)} %constant.140.clone.1..sunk.1, s32[]{:T(128)} %constant.140.clone.1..sunk.1) | dynamic-update-slice | bytes 1572868 | tf_op jit(solution)/shard_map/transpose(jvp())/while/body/jit(dynamic_update_index_in_dim)/dynamic_update_slice | solution.py:74
  334.7 4.3 fusion.252
  343.6 17.9 %dynamic_update_slice.69 = f32[4,256,12,64]{1,0,3,2:T(4,128)} dynamic-update-slice(f32[4,256,12,64]{1,0,3,2:T(4,128)} %get-tuple-element.1274, f32[1,256,12,64]{1,0,3,2:T(1,128)S(1)} %copy.305, s32[]{:T(128)S(6)} %sub.287, s32[]{:T(128)} %constant.140.clone.1..sunk.1, s32[]{:T(128)} %constant.140.clone.1..sunk.1, s32[]{:T(128)} %constant.140.clone.1..sunk.1) | dynamic-update-slice | bytes 1572868 | tf_op jit(solution)/shard_map/transpose(jvp())/while/body/jit(dynamic_update_index_in_dim)/dynamic_update_slice | solution.py:74
  389.1 4.3 fusion.252
  398.0 17.9 %dynamic_update_slice.69 = f32[4,256,12,64]{1,0,3,2:T(4,128)} dynamic-update-slice(f32[4,256,12,64]{1,0,3,2:T(4,128)} %get-tuple-element.1274, f32[1,256,12,64]{1,0,3,2:T(1,128)S(1)} %copy.305, s32[]{:T(128)S(6)} %sub.287, s32[]{:T(128)} %constant.140.clone.1..sunk.1, s32[]{:T(128)} %constant.140.clone.1..sunk.1, s32[]{:T(128)} %constant.140.clone.1..sunk.1) | dynamic-update-slice | bytes 1572868 | tf_op jit(solution)/shard_map/transpose(jvp())/while/body/jit(dynamic_update_index_in_dim)/dynamic_update_slice | solution.py:74
  452.3 17.9 %dynamic_update_slice.69 = f32[4,256,12,64]{1,0,3,2:T(4,128)} dynamic-update-slice(f32[4,256,12,64]{1,0,3,2:T(4,128)} %get-tuple-element.1274, f32[1,256,12,64]{1,0,3,2:T(1,128)S(1)} %copy.305, s32[]{:T(128)S(6)} %sub.287, s32[]{:T(128)} %constant.140.clone.1..sunk.1, s32[]{:T(128)} %constant.140.clone.1..sunk.1, s32[]{:T(128)} %constant.140.clone.1..sunk.1) | dynamic-update-slice | bytes 1572868 | tf_op jit(solution)/shard_map/transpose(jvp())/while/body/jit(dynamic_update_index_in_dim)/dynamic_update_slice | solution.py:74
  488.0 10.9 %multiply_reduce_fusion.8 = (f32[1024]{0:T(1024)S(1)}, f32[1024]{0:T(1024)S(1)}, f32[1024]{0:T(1024)S(1)}, f32[1024]{0:T(1024)S(1)}, f32[1024]{0:T(1024)S(1)}, /*index=5*/f32[1024,1024]{0,1:T(8,128)S(1)}) fusion(f32[1024,1024]{0,1:T(8,128)} %copy-done, f32[1024]{0:T(1024)S(1)} %copy-done.43, f32[1024]{0:T(1024)S(1)} %copy-done.41, f32[1024]{0:T(1024)S(1)} %copy-done.39, ...), kind=kLoop, calls=%fused_computation.154 | loop fusion | flops 25160704 | bytes 21004288 | tf_op jit(solution)/shard_map/transpose(jvp())/reduce_sum | solution.py:27
  507.5 4.6 fusion.112
  540.8 8.7 %collective-permute-done.6 = bf16[512,256]{0,1:T(8,128)(2,1)S(1)} collective-permute-done((bf16[512,256]{0,1:T(8,128)(2,1)S(1)}, bf16[512,256]{0,1:T(8,128)(2,1)S(1)}, u32[]{:S(2)}, u32[]{:S(2)}) %collective-permute-start.6) | collective-permute-done | bytes 262176 | tf_op jit(solution)/shard_map/ppermute | solution.py:337
  555.0 56.0 %scatter_rows.1 = (f32[48,2688]{1,0:T(8,128)}, f32[24,256]{1,0:T(8,128)}, f32[16,768]{1,0:T(8,128)}) custom-call(bf16[16,48,2688]{2,1,0:T(8,128)(2,1)} %constant_dynamic-update-slice_fusion.7.refs_0_, f32[16,768]{1,0:T(8,128)} %concatenate.80.refs_1_), custom_call_target="tpu_custom_call" | custom-call | tf_op jit(solution)/shard_map/scatter_rows/pallas_call | solution.py:307
  (708 shorter events, 301.5 us)
Async XLA Ops:
  0.6 19.1 %collective-permute-start.1 = (bf16[24,256]{1,0:T(8,128)(2,1)}, bf16[24,256]{1,0:T(8,128)(2,1)S(1)}, u32[]{:S(2)}, u32[]{:S(2)}) collective-permute-start(bf16[24,256]{1,0:T(8,128)(2,1)} %param.26), channel_id=1, source_target_pairs={{0,1},{1,0},{2,3},{3,2},{4,5},{5,4},{6,7},{7,6},{8,9},{9,8},{10,11... | collective-permute-start | bytes 36872 | tf_op jit(solution)/shard_map/ppermute | solution.py:337
  7.0 54.7 %copy-start.16 = (bf16[512,768]{1,0:T(8,128)(2,1)}, bf16[512,768]{1,0:T(8,128)(2,1)S(1)}, u32[]{:S(2)}) copy-start(bf16[512,768]{1,0:T(8,128)(2,1)S(1)} %fusion.103) | copy-start | bytes 2359300
  7.0 51.7 %collective-permute-start = (bf16[512,768]{1,0:T(8,128)(2,1)S(1)}, bf16[512,768]{1,0:T(8,128)(2,1)S(1)}, u32[]{:S(2)}, u32[]{:S(2)}) collective-permute-start(bf16[512,768]{1,0:T(8,128)(2,1)S(1)} %fusion.103), channel_id=1, source_target_pairs={{0,1},{1,0},{2,3},{3,2},{4,5},{5,4},{6,7},{7,6},{8,9},{9,8},{10,11... | collective-permute-start | bytes 2359304 | tf_op jit(solution)/shard_map/ppermute | solution.py:337
  7.1 223.9 %collective-permute-start.2 = (bf16[512,768]{1,0:T(8,128)(2,1)}, bf16[512,768]{1,0:T(8,128)(2,1)}, u32[]{:S(2)}, u32[]{:S(2)}) collective-permute-start(bf16[512,768]{1,0:T(8,128)(2,1)} %param.37), channel_id=1, source_target_pairs={{0,1},{1,0},{2,3},{3,2},{4,5},{5,4},{6,7},{7,6},{8,9},{9,8},{10,11... | collective-permute-start | bytes 2359304 | tf_op jit(solution)/shard_map/ppermute | solution.py:337
  11.6 53.1 %copy-start.38 = (f32[1024]{0:T(1024)}, f32[1024]{0:T(1024)S(1)}, u32[]{:S(2)}) copy-start(f32[1024]{0:T(1024)S(1)} %get-tuple-element.959) | copy-start | bytes 12292
  11.6 53.1 %copy-start.40 = (f32[1024]{0:T(1024)}, f32[1024]{0:T(1024)S(1)}, u32[]{:S(2)}) copy-start(f32[1024]{0:T(1024)S(1)} %get-tuple-element.960) | copy-start | bytes 12292
  11.6 53.1 %copy-start.42 = (f32[1024]{0:T(1024)}, f32[1024]{0:T(1024)S(1)}, u32[]{:S(2)}) copy-start(f32[1024]{0:T(1024)S(1)} %get-tuple-element.961) | copy-start | bytes 12292
  17.5 47.1 %copy-start.51 = (f32[1,1024]{1,0:T(1,128)}, f32[1,1024]{1,0:T(1,128)S(1)}, u32[]{:S(2)}) copy-start(f32[1,1024]{1,0:T(1,128)S(1)} %get-tuple-element.953) | copy-start | bytes 12292
  17.6 47.1 %copy-start.53 = (f32[1,1024]{1,0:T(1,128)}, f32[1,1024]{1,0:T(1,128)S(1)}, u32[]{:S(2)}) copy-start(f32[1,1024]{1,0:T(1,128)S(1)} %get-tuple-element.954) | copy-start | bytes 12292
  17.6 47.1 %copy-start.55 = (f32[1,1024]{1,0:T(1,128)}, f32[1,1024]{1,0:T(1,128)S(1)}, u32[]{:S(2)}) copy-start(f32[1,1024]{1,0:T(1,128)S(1)} %get-tuple-element.955) | copy-start | bytes 12292
  17.6 47.1 %copy-start.57 = (f32[1,1024]{1,0:T(1,128)}, f32[1,1024]{1,0:T(1,128)S(1)}, u32[]{:S(2)}) copy-start(f32[1,1024]{1,0:T(1,128)S(1)} %get-tuple-element.956) | copy-start | bytes 12292
  19.8 224.8 %copy-start.49 = (f32[768]{0:T(1024)}, f32[768]{0:T(1024)S(1)}, u32[]{:S(2)}) copy-start(f32[768]{0:T(1024)S(1)} %mul.839) | copy-start | bytes 9220
  240.8 3.7 collective-permute-start.3
  287.2 22.2 %copy-start.47 = (f32[12]{0:T(128)S(1)}, f32[12]{0:T(128)}, u32[]{:S(2)}) copy-start(f32[12]{0:T(128)} %get-tuple-element.1200) | copy-start | bytes 148 | tf_op jit(solution)/shard_map/transpose(jvp())/while
  289.3 21.0 %copy-start.32 = (f32[256]{0:T(256)S(1)}, f32[256]{0:T(256)}, u32[]{:S(2)}) copy-start(f32[256]{0:T(256)} %copy-done.31) | copy-start | bytes 3076 | tf_op jit(solution)/shard_map/transpose(jvp())/while
  341.5 22.2 %copy-start.47 = (f32[12]{0:T(128)S(1)}, f32[12]{0:T(128)}, u32[]{:S(2)}) copy-start(f32[12]{0:T(128)} %get-tuple-element.1200) | copy-start | bytes 148 | tf_op jit(solution)/shard_map/transpose(jvp())/while
  343.6 21.0 %copy-start.32 = (f32[256]{0:T(256)S(1)}, f32[256]{0:T(256)}, u32[]{:S(2)}) copy-start(f32[256]{0:T(256)} %copy-done.31) | copy-start | bytes 3076 | tf_op jit(solution)/shard_map/transpose(jvp())/while
  395.9 22.2 %copy-start.47 = (f32[12]{0:T(128)S(1)}, f32[12]{0:T(128)}, u32[]{:S(2)}) copy-start(f32[12]{0:T(128)} %get-tuple-element.1200) | copy-start | bytes 148 | tf_op jit(solution)/shard_map/transpose(jvp())/while
  450.2 22.2 %copy-start.47 = (f32[12]{0:T(128)S(1)}, f32[12]{0:T(128)}, u32[]{:S(2)}) copy-start(f32[12]{0:T(128)} %get-tuple-element.1200) | copy-start | bytes 148 | tf_op jit(solution)/shard_map/transpose(jvp())/while
  523.1 28.3 %collective-permute-start.5 = (bf16[512,768]{1,0:T(8,128)(2,1)}, bf16[512,768]{1,0:T(8,128)(2,1)}, u32[]{:S(2)}, u32[]{:S(2)}) collective-permute-start(bf16[512,768]{1,0:T(8,128)(2,1)} %dynamic-slice_convert_fusion), channel_id=1, source_target_pairs={{0,1},{1,0},{2,3},{3,2},{4,5},{5,4},{6,7},{7,6},{8,9},{9,8},{10,11... | collective-permute-start | bytes 2359304 | tf_op jit(solution)/shard_map/ppermute | solution.py:337
  523.7 25.7 %collective-permute-start.6 = (bf16[512,256]{0,1:T(8,128)(2,1)S(1)}, bf16[512,256]{0,1:T(8,128)(2,1)S(1)}, u32[]{:S(2)}, u32[]{:S(2)}) collective-permute-start(bf16[512,256]{0,1:T(8,128)(2,1)S(1)} %dynamic-slice_convert_fusion.2), channel_id=1, source_target_pairs={{0,1},{1,0},{2,3},{3,2},{4,5},{5,4},{6,7},{7,6},{8,9},{9,8},{10,11... | collective-permute-start | bytes 786440 | tf_op jit(solution)/shard_map/ppermute | solution.py:337
  530.8 90.2 %collective-permute-start.4 = (bf16[512,768]{1,0:T(8,128)(2,1)}, bf16[512,768]{1,0:T(8,128)(2,1)}, u32[]{:S(2)}, u32[]{:S(2)}) collective-permute-start(bf16[512,768]{1,0:T(8,128)(2,1)} %dynamic-slice_convert_fusion.1), channel_id=1, source_target_pairs={{0,1},{1,0},{2,3},{3,2},{4,5},{5,4},{6,7},{7,6},{8,9},{9,8},{10,11... | collective-permute-start | bytes 2359304 | tf_op jit(solution)/shard_map/ppermute | solution.py:337
  553.7 67.3 %copy-start.28 = (bf16[512,768]{1,0:T(8,128)(2,1)S(1)}, bf16[512,768]{1,0:T(8,128)(2,1)}, u32[]{:S(2)}) copy-start(bf16[512,768]{1,0:T(8,128)(2,1)} %param.37) | copy-start | bytes 2359300
  553.7 67.3 %copy-start.70 = (f32[512]{0:T(512)S(1)}, f32[512]{0:T(512)}, u32[]{:S(2)}) copy-start(f32[512]{0:T(512)} %get-tuple-element.962) | copy-start | bytes 6148
  (102 other events, 588.9 us)

commit v2 on v1

--- a/solution.py
+++ b/solution.py
@@ -26,85 +26,6 @@
         same_doc = (seg_pad[first_row : first_row + length] == seg_row).astype(stream.dtype)
         summed = summed + weight[width - 1 - shift_by][None, :] * window * same_doc[:, None]
     return summed
-
-
-def block_scan_state(values, b_rows, c_rows, step_rows, seg_row, decay_rate):
-    length, head_count, head_size = values.shape
-    state_width = b_rows.shape[1]
-    blocks = length // GROUP
-    seg_blocks = seg_row.reshape(blocks, GROUP)
-    prev_segs = jnp.concatenate([jnp.full((1,), -1, jnp.int32), seg_blocks[:-1, GROUP - 1]], 0)
-    causal = jnp.arange(GROUP)[:, None] >= jnp.arange(GROUP)[None, :]
-
-    def scan_step(carried, block_item):
-        x_block, b_block, c_block, dt_block, seg_block, prev_seg = block_item
-        cum_rate = jnp.cumsum(dt_block * decay_rate[None, :], axis=0)
-        keep_mask = causal & (seg_block[:, None] == seg_block[None, :])
-        exponent = jnp.where(
-            keep_mask[None], cum_rate.T[:, :, None] - cum_rate.T[:, None, :], -jnp.inf
-        )
-        decay_in = jnp.exp(exponent)
-        scores = jnp.dot(c_block, b_block.T, precision=HIGH)
-        mixing = scores[None] * decay_in
-        x_scaled = x_block * dt_block[:, :, None]
-        y_inner = jnp.einsum("hts,shp->thp", mixing, x_scaled, precision=HIGH)
-        carry_ok = (seg_block == prev_seg).astype(values.dtype)
-        y_state = jnp.einsum("tn,hnp->thp", c_block, carried, precision=HIGH)
-        y_state = y_state * (jnp.exp(cum_rate) * carry_ok[:, None])[:, :, None]
-        block_total = cum_rate[GROUP - 1]
-        tail_decay = (
-            jnp.exp(block_total[None, :] - cum_rate)
-            * (seg_block == seg_block[GROUP - 1]).astype(values.dtype)[:, None]
-        )
-        keep_state = jnp.exp(block_total) * (seg_block[GROUP - 1] == prev_seg).astype(values.dtype)
-        new_state = carried * keep_state[:, None, None] + jnp.einsum(
-            "sn,shp->hnp", b_block, x_scaled * tail_decay[:, :, None], precision=HIGH
-        )
-        return (new_state, y_inner + y_state)
-
-    start_state = jnp.zeros((head_count, state_width, head_size), values.dtype)
-    block_inputs = (
-        values.reshape(blocks, GROUP, head_count, head_size),
-        b_rows.reshape(blocks, GROUP, state_width),
-        c_rows.reshape(blocks, GROUP, state_width),
-        step_rows.reshape(blocks, GROUP, head_count),
-        seg_blocks,
-        prev_segs,
-    )
-    final_state, outputs = lax.scan(jax.checkpoint(scan_step), start_state, block_inputs)
-    return (outputs.reshape(length, head_count, head_size), final_state)
-
-
-def mixer(
-    pre_gate,
-    pre_value,
-    pre_bc,
-    pre_step,
-    conv_value,
-    conv_bc,
-    conv_value_bias,
-    conv_bc_bias,
-    step_bias,
-    decay_log,
-    skip_gain,
-    seg_row,
-):
-    length, inner_width = pre_value.shape
-    head_count = pre_step.shape[1]
-    head_size = inner_width // head_count
-    state_width = pre_bc.shape[1] // 2
-    stream = jnp.concatenate([pre_value, pre_bc], 1)
-    taps = jnp.concatenate([conv_value, conv_bc], 1)
-    offset = jnp.concatenate([conv_value_bias, conv_bc_bias], 0)
-    activated = jax.nn.silu(conv_mix(stream, taps, offset, seg_row))
-    values = activated[:, :inner_width].reshape(length, head_count, head_size)
-    b_rows = activated[:, inner_width : inner_width + state_width]
-    c_rows = activated[:, inner_width + state_width :]
-    step_rows = jax.nn.softplus(pre_step + step_bias[None, :])
-    decay_rate = -jnp.exp(decay_log)
-    scanned, _ = block_scan_state(values, b_rows, c_rows, step_rows, seg_row, decay_rate)
-    ssm_out = scanned + skip_gain[None, :, None] * values
-    return ssm_out.reshape(length, inner_width) * jax.nn.silu(pre_gate)
 
 
 def contract_rows(left, right):
@@ -349,6 +270,333 @@
     away = lax.dynamic_slice_in_dim(values, (1 - index) * span, span, 0)
     kept = lax.dynamic_slice_in_dim(values, index * span, span, 0)
     return kept + swap(away.astype(jnp.bfloat16)).astype(jnp.float32)
+
+
+def mm(left, right, left_dim, right_dim, both=True):
+    def one(first, second):
+        return lax.dot_general(
+            first,
+            second,
+            (((left_dim,), (right_dim,)), ((), ())),
+            preferred_element_type=jnp.float32,
+        )
+
+    def split(values):
+        high = values.astype(jnp.bfloat16)
+        return high, (values - high.astype(jnp.float32)).astype(jnp.bfloat16)
+
+    left_high, left_low = split(left)
+    right_high, right_low = split(right)
+    if not both:
+        return one(left_high, right_high)
+    return one(left_high, right_high) + (one(left_high, right_low) + one(left_low, right_high))
+
+
+def shifted(values, by):
+    if by == 0:
+        return values
+    return pltpu.roll(values, by % values.shape[0], 0)
+
+
+def conv_pair(stream, masks, taps_ref, offset_ref):
+    width = taps_ref.shape[0]
+    summed = offset_ref[...] + taps_ref[width - 1 : width, :] * stream
+    for by in range(1, width):
+        window = shifted(stream, by) * masks[:, by - 1 : by]
+        summed = summed + taps_ref[width - 1 - by : width - by, :] * window
+    return summed
+
+
+def pair_cols(first, second, span, head_size):
+    lane = lax.broadcasted_iota(jnp.int32, (span, 2 * head_size), 1)
+    return jnp.where(lane < head_size, first, second)
+
+
+def keep_pairs(seg_col, seg_row):
+    span = seg_col.shape[0]
+    later = lax.broadcasted_iota(jnp.int32, (span, span), 0)
+    earlier = lax.broadcasted_iota(jnp.int32, (span, span), 1)
+    return (later >= earlier) & (seg_col == seg_row)
+
+
+def block_terms(block, cols_ref, masks_ref, head_size):
+    rows = pl.ds(block * GROUP, GROUP)
+    cum0, cum1 = cols_ref[0, rows, 0:1], cols_ref[0, rows, 1:2]
+    last = pl.ds(block * GROUP + GROUP - 1, 1)
+    tot0, tot1 = cols_ref[0, last, 0:1], cols_ref[0, last, 1:2]
+    step = pair_cols(cols_ref[0, rows, 2:3], cols_ref[0, rows, 3:4], GROUP, head_size)
+    tail = jnp.exp(pair_cols(tot0 - cum0, tot1 - cum1, GROUP, head_size)) * masks_ref[rows, 4:5]
+    enter = jnp.exp(pair_cols(cum0, cum1, GROUP, head_size)) * masks_ref[rows, 3:4]
+    keep = jnp.exp(pair_cols(tot0, tot1, 1, head_size)) * masks_ref[last, 5:6]
+    return rows, cum0, cum1, step, tail, enter, keep
+
+
+def forward_kernel(
+    head_size,
+    value_ref,
+    gate_ref,
+    branch_ref,
+    bc_ref,
+    cols_ref,
+    rows_ref,
+    masks_ref,
+    seg_col_ref,
+    seg_row_ref,
+    taps_ref,
+    offset_ref,
+    skip_ref,
+    gain_ref,
+    gated_ref,
+    ssm_ref,
+    states_ref,
+    sums_ref,
+    scores,
+    mixed_x,
+):
+    length, state_width = value_ref.shape[0], bc_ref.shape[1] // 2
+    first = pl.program_id(0) == 0
+
+    @pl.when(first)
+    def _():
+        sums_ref[...] = jnp.zeros_like(sums_ref)
+        for block in range(length // GROUP):
+            rows = pl.ds(block * GROUP, GROUP)
+            raw = mm(bc_ref[rows, state_width:], bc_ref[rows, :state_width], 1, 1)
+            scores[block] = jnp.where(keep_pairs(seg_col_ref[rows, :], seg_row_ref[:, rows]), raw, 0.0)
+
+    conv = conv_pair(value_ref[...], masks_ref[...], taps_ref, offset_ref)
+    mixed_x[...] = conv * jax.nn.sigmoid(conv)
+    state = jnp.zeros((state_width, 2 * head_size), jnp.float32)
+    for block in range(length // GROUP):
+        rows, cum0, cum1, step, tail, enter, keep = block_terms(
+            block, cols_ref, masks_ref, head_size
+        )
+        x = mixed_x[rows, :]
+        x_step = x * step
+        score = scores[block]
+        mix0 = score * jnp.exp(jnp.minimum(cum0 - rows_ref[0, 0:1, rows], 0.0))
+        mix1 = score * jnp.exp(jnp.minimum(cum1 - rows_ref[0, 1:2, rows], 0.0))
+        y = pair_cols(
+            mm(mix0, x_step, 1, 0),
+            mm(mix1, x_step, 1, 0),
+            GROUP,
+            head_size,
+        )
+        states_ref[0, block] = state
+        if block > 0:
+            y = y + mm(bc_ref[rows, state_width:], state, 1, 0) * enter
+        grown = mm(bc_ref[rows, :state_width], (x_step * tail), 0, 0)
+        state = state * keep + grown
+        ssm = y + skip_ref[...] * x
+        gate = gate_ref[rows, :]
+        gated = ssm * (gate * jax.nn.sigmoid(gate))
+        ssm_ref[rows, :] = ssm
+        gated_ref[rows, :] = gated
+        sums_ref[rows, 0:1] += jnp.sum(gated * gated, 1, keepdims=True)
+        weighted = branch_ref[rows, :] * gain_ref[...]
+        sums_ref[rows, 1:2] += jnp.sum(gated * weighted, 1, keepdims=True)
+
+
+def backward_kernel(
+    head_size,
+    value_ref,
+    gate_ref,
+    branch_ref,
+    ssm_ref,
+    states_ref,
+    norm_ref,
+    bc_ref,
+    cols_ref,
+    rows_ref,
+    masks_ref,
+    seg_col_ref,
+    seg_row_ref,
+    taps_ref,
+    offset_ref,
+    skip_ref,
+    gain_ref,
+    grad_gate_ref,
+    grad_value_ref,
+    grad_bc_ref,
+    grad_cols_ref,
+    params_ref,
+    scores,
+    grad_scores,
+    mixed_x,
+    slope,
+    grad_y,
+):
+    length, state_width = value_ref.shape[0], bc_ref.shape[1] // 2
+    blocks = length // GROUP
+    width = taps_ref.shape[0]
+
+    @pl.when(pl.program_id(0) == 0)
+    def _():
+        grad_bc_ref[...] = jnp.zeros_like(grad_bc_ref)
+        grad_scores[...] = jnp.zeros_like(grad_scores)
+        for block in range(blocks):
+            rows = pl.ds(block * GROUP, GROUP)
+            raw = mm(bc_ref[rows, state_width:], bc_ref[rows, :state_width], 1, 1)
+            scores[block] = jnp.where(keep_pairs(seg_col_ref[rows, :], seg_row_ref[:, rows]), raw, 0.0)
+
+    conv = conv_pair(value_ref[...], masks_ref[...], taps_ref, offset_ref)
+    sig = jax.nn.sigmoid(conv)
+    mixed_x[...] = conv * sig
+    slope[...] = sig * (1.0 + conv * (1.0 - sig))
+    gate = gate_ref[...]
+    gate_sig = jax.nn.sigmoid(gate)
+    ssm = ssm_ref[...]
+    gated = ssm * (gate * gate_sig)
+    inv_gate = norm_ref[:, 0:1]
+    branch = branch_ref[...]
+    grad_gated = inv_gate * (branch * gain_ref[...]) - gated * norm_ref[:, 1:2]
+    grad_gate_ref[...] = (
+        grad_gated * ssm * (gate_sig * (1.0 + gate * (1.0 - gate_sig)))
+    ).astype(jnp.bfloat16)
+    grad_y[...] = grad_gated * (gate * gate_sig)
+    params_ref[0, 5:6, :] = jnp.sum(branch * gated * inv_gate, 0, keepdims=True)
+    params_ref[0, 6:7, :] = jnp.sum(grad_y[...] * mixed_x[...], 0, keepdims=True)
+    lane = lax.broadcasted_iota(jnp.int32, (GROUP, 2 * head_size), 1)
+    at_last = lax.broadcasted_iota(jnp.int32, (GROUP, 1), 0) == GROUP - 1
+
+    def head_sums(values):
+        return (
+            jnp.sum(jnp.where(lane < head_size, values, 0.0), 1, keepdims=True),
+            jnp.sum(jnp.where(lane < head_size, 0.0, values), 1, keepdims=True),
+        )
+
+    grad_state = jnp.zeros((state_width, 2 * head_size), jnp.float32)
+    for block in reversed(range(blocks)):
+        rows, cum0, cum1, step, tail, enter, keep = block_terms(
+            block, cols_ref, masks_ref, head_size
+        )
+        b_rows, c_rows = bc_ref[rows, :state_width], bc_ref[rows, state_width:]
+        x = mixed_x[rows, :]
+        dy = grad_y[rows, :]
+        x_step = x * step
+        score = scores[block]
+        decay0 = jnp.exp(jnp.minimum(cum0 - rows_ref[0, 0:1, rows], 0.0))
+        decay1 = jnp.exp(jnp.minimum(cum1 - rows_ref[0, 1:2, rows], 0.0))
+        dy0 = jnp.where(lane < head_size, dy, 0.0)
+        dy1 = jnp.where(lane < head_size, 0.0, dy)
+        grad_scores[block] += mm(dy0, x_step, 1, 1) * decay0 + mm(dy1, x_step, 1, 1) * decay1
+        inner = mm((score * decay0), dy0, 0, 0) + mm(
+            (score * decay1), dy1, 0, 0
+        )
+        state = states_ref[0, block]
+        grad_low = grad_state
+        from_state = mm(b_rows, grad_low, 1, 0)
+        x_tail = x_step * tail
+        grad_bc_ref[rows, :state_width] += mm(x_tail, grad_low, 1, 1)
+        grad_xs = inner + from_state * tail
+        crossing = from_state * x_tail
+        total = jnp.sum(crossing, 0, keepdims=True) + keep * jnp.sum(
+            state * grad_state, 0, keepdims=True
+        )
+        y = ssm_ref[rows, :] - skip_ref[...] * x
+        per_token = dy * y - x_step * inner - crossing
+        sum0, sum1 = head_sums(jnp.where(at_last, per_token + total, per_token))
+        grad_cols_ref[0, rows, 0:1] = sum0
+        grad_cols_ref[0, rows, 1:2] = sum1
+        step0, step1 = head_sums(grad_xs * x)
+        grad_cols_ref[0, rows, 2:3] = step0
+        grad_cols_ref[0, rows, 3:4] = step1
+        grad_state = grad_state * keep
+        if block > 0:
+            dy_state = (dy * enter)
+            grad_bc_ref[rows, state_width:] += mm(dy_state, state, 1, 1)
+            grad_state = grad_state + mm(c_rows, dy_state, 0, 0)
+        grad_y[rows, :] = (grad_xs * step + skip_ref[...] * dy) * slope[rows, :]
+
+    grad_conv = grad_y[...]
+    stream = value_ref[...]
+    masks = masks_ref[...]
+    grad_stream = taps_ref[width - 1 : width, :] * grad_conv
+    params_ref[0, width - 1 : width, :] = jnp.sum(grad_conv * stream, 0, keepdims=True)
+    params_ref[0, 4:5, :] = jnp.sum(grad_conv, 0, keepdims=True)
+    params_ref[0, 7:8, :] = jnp.zeros_like(skip_ref)
+    for by in range(1, width):
+        tap = width - 1 - by
+        kept = grad_conv * masks[:, by - 1 : by]
+        grad_stream = grad_stream + taps_ref[tap : tap + 1, :] * shifted(kept, -by)
+        params_ref[0, tap : tap + 1, :] = jnp.sum(kept * shifted(stream, by), 0, keepdims=True)
+    grad_value_ref[...] = grad_stream.astype(jnp.bfloat16)
+
+    @pl.when(pl.program_id(0) == pl.num_programs(0) - 1)
+    def _():
+        for block in range(blocks):
+            rows = pl.ds(block * GROUP, GROUP)
+            b_rows, c_rows = bc_ref[rows, :state_width], bc_ref[rows, state_width:]
+            kept = keep_pairs(seg_col_ref[rows, :], seg_row_ref[:, rows])
+            grad = jnp.where(kept, grad_scores[block], 0.0)
+            grad_bc_ref[rows, state_width:] += mm(grad, b_rows, 1, 0)
+            grad_bc_ref[rows, :state_width] += mm(grad, c_rows, 0, 0)
+
+
+def mixer_calls(length, inner, head_size, state_width):
+    pairs = inner // (2 * head_size)
+    blocks = length // GROUP
+    lanes = 2 * head_size
+    f32 = jnp.float32
+    wide = pl.BlockSpec((length, lanes), lambda i: (0, i))
+    states = pl.BlockSpec((1, blocks, state_width, lanes), lambda i: (i, 0, 0, 0))
+
+    def whole(*shape):
+        return pl.BlockSpec(shape, lambda i: (0,) * len(shape))
+
+    common = [
+        whole(length, 2 * state_width),
+        pl.BlockSpec((1, length, 4), lambda i: (i, 0, 0)),
+        pl.BlockSpec((1, 2, length), lambda i: (i, 0, 0)),
+        whole(length, 8),
+        whole(length, 1),
+        whole(1, length),
+        pl.BlockSpec((4, lanes), lambda i: (0, i)),
+        pl.BlockSpec((1, lanes), lambda i: (0, i)),
+        pl.BlockSpec((1, lanes), lambda i: (0, i)),
+        pl.BlockSpec((1, lanes), lambda i: (0, i)),
+    ]
+    square = pltpu.VMEM((blocks, GROUP, GROUP), f32)
+    column = pltpu.VMEM((length, lanes), f32)
+    params = pltpu.CompilerParams(vmem_limit_bytes=VMEM_LIMIT)
+    forward = pl.pallas_call(
+        lambda *refs: forward_kernel(head_size, *refs),
+        grid=(pairs,),
+        in_specs=[wide, wide, wide] + common,
+        out_specs=(wide, wide, states, whole(length, 2)),
+        out_shape=(
+            jax.ShapeDtypeStruct((length, inner), f32),
+            jax.ShapeDtypeStruct((length, inner), f32),
+            jax.ShapeDtypeStruct((pairs, blocks, state_width, lanes), f32),
+            jax.ShapeDtypeStruct((length, 2), f32),
+        ),
+        scratch_shapes=[square, column],
+        compiler_params=params,
+        name="mixer_forward",
+    )
+    backward = pl.pallas_call(
+        lambda *refs: backward_kernel(head_size, *refs),
+        grid=(pairs,),
+        in_specs=[wide, wide, wide, wide, states, whole(length, 2)] + common,
+        out_specs=(
+            wide,
+            wide,
+            whole(length, 2 * state_width),
+            pl.BlockSpec((1, length, 4), lambda i: (i, 0, 0)),
+            pl.BlockSpec((1, 8, lanes), lambda i: (i, 0, 0)),
+        ),
+        out_shape=(
+            jax.ShapeDtypeStruct((length, inner), jnp.bfloat16),
+            jax.ShapeDtypeStruct((length, inner), jnp.bfloat16),
+            jax.ShapeDtypeStruct((length, 2 * state_width), f32),
+            jax.ShapeDtypeStruct((pairs, length, 4), f32),
+            jax.ShapeDtypeStruct((pairs, 8, lanes), f32),
+        ),
+        scratch_shapes=[square, square, column, column, column],
+        compiler_params=params,
+        name="mixer_backward",
+    )
+    return forward, backward
 
 
 def local(
@@ -404,50 +652,82 @@
     pre_bc = jnp.dot(rows_all, bc_full, preferred_element_type=jnp.float32)
     pre_step = jnp.dot(rows_all, step_full, preferred_element_type=jnp.float32)[:, :head_count]
     grad_branch = jnp.dot(cot_all, outw_full, preferred_element_type=jnp.float32)
-    weighted = grad_branch * gate_gain[None, :]
-
-    def local_mixer(*inputs):
-        return mixer(*inputs, segments.reshape(-1))
-
-    gated, pull_back = jax.vjp(
-        local_mixer,
-        pre_gate,
-        pre_value,
-        pre_bc,
-        pre_step,
+    seg_row = segments.reshape(length)
+    blocks = length // GROUP
+    head_size = inner // head_count
+    pairs = head_count // 2
+    forward, backward = mixer_calls(length, inner, head_size, bc_width // 2)
+
+    def mix_bc(stream, taps, offset):
+        return jax.nn.silu(conv_mix(stream, taps, offset, seg_row))
+
+    bc_act, pull_bc = jax.vjp(mix_bc, pre_bc, conv_bc, conv_bc_bias)
+    shifted_step = pre_step + step_bias[None, :]
+    step_rows = jax.nn.softplus(shifted_step)
+    decay_rate = -jnp.exp(decay_log)
+    triangle = jnp.tril(jnp.ones((GROUP, GROUP), jnp.float32))
+    rate_blocks = (step_rows * decay_rate[None, :]).reshape(blocks, GROUP, head_count)
+    cum = jnp.einsum("ts,bsh->bth", triangle, rate_blocks, precision=HIGH)
+    cum = cum.reshape(length, head_count)
+    by_pair = jnp.concatenate(
+        [cum.reshape(length, pairs, 2), step_rows.reshape(length, pairs, 2)], 2
+    ).transpose(1, 0, 2)
+    cum_rows = cum.T.reshape(pairs, 2, length)
+    seg_blocks = seg_row.reshape(blocks, GROUP)
+    seg_last = seg_blocks[:, GROUP - 1]
+    prev_last = jnp.concatenate([jnp.full((1,), -1, jnp.int32), seg_last[:-1]], 0)
+    masks = [
+        jnp.concatenate([jnp.zeros((by,), bool), seg_row[by:] == seg_row[:-by]], 0)
+        for by in range(1, 4)
+    ]
+    masks += [
+        (seg_blocks == prev_last[:, None]).reshape(length),
+        (seg_blocks == seg_last[:, None]).reshape(length),
+        jnp.broadcast_to((seg_last == prev_last)[:, None], (blocks, GROUP)).reshape(length),
+    ]
+    masks += [jnp.zeros((length,), bool)] * 2
+    common = (
+        bc_act,
+        by_pair,
+        cum_rows,
+        jnp.stack(masks, 1).astype(jnp.float32),
+        seg_row[:, None],
+        seg_row[None, :],
         conv_value,
-        conv_bc,
-        conv_value_bias,
-        conv_bc_bias,
-        step_bias,
-        decay_log,
-        skip_gain,
-    )
-    sums = jnp.stack([jnp.sum(gated * gated, -1), jnp.sum(weighted * gated, -1)], 0)
-    sums = sums + swap(sums)
-    inv_gate = lax.rsqrt(sums[0] / DI + EPS)[:, None]
-    cross = (sums[1] / DI)[:, None]
+        conv_value_bias[None, :],
+        jnp.repeat(skip_gain, head_size)[None, :],
+        gate_gain[None, :],
+    )
+    gated, ssm_out, states, sums = forward(pre_value, pre_gate, grad_branch, *common)
+    sums = (sums.T + swap(sums.T)).T
+    inv_gate = lax.rsqrt(sums[:, :1] / DI + EPS)
+    pull_scale = inv_gate**3 * (sums[:, 1:] / DI)
     branch_in = (gated * inv_gate * gate_gain[None, :]).astype(jnp.bfloat16)
     branch = own_half(contract_cols(branch_in, outw_full), own_index)
     mixed_out = (residual + branch).astype(jnp.bfloat16)
     grad_out_w = contract_rows(cot_all, branch_in)
-    grad_gate_gain = jnp.sum(grad_branch * gated * inv_gate, 0)
-    grad_gated = inv_gate * weighted - gated * inv_gate**3 * cross
-    (
-        grad_pg,
-        grad_pv,
-        grad_pbc,
-        grad_ps,
-        grad_cv,
-        grad_cbc,
-        grad_cvb,
-        grad_cbcb,
-        grad_sb,
-        grad_dl,
-        grad_sk,
-    ) = pull_back(grad_gated)
-    low_gate = grad_pg.astype(jnp.bfloat16)
-    low_value = grad_pv.astype(jnp.bfloat16)
+    low_gate, low_value, grad_bc_act, grad_cols, params = backward(
+        pre_value,
+        pre_gate,
+        grad_branch,
+        ssm_out,
+        states,
+        jnp.concatenate([inv_gate, pull_scale], 1),
+        *common,
+    )
+    grad_pbc, grad_cbc, grad_cbcb = pull_bc(grad_bc_act)
+    grad_cum = grad_cols[:, :, :2].transpose(1, 0, 2).reshape(blocks, GROUP, head_count)
+    grad_direct = grad_cols[:, :, 2:].transpose(1, 0, 2).reshape(length, head_count)
+    grad_rate = jnp.einsum("ts,bth->bsh", triangle, grad_cum, precision=HIGH)
+    grad_rate = grad_rate.reshape(length, head_count)
+    grad_ps = (grad_rate * decay_rate[None, :] + grad_direct) * jax.nn.sigmoid(shifted_step)
+    grad_sb = jnp.sum(grad_ps, 0)
+    grad_dl = jnp.sum(grad_rate * step_rows, 0) * decay_rate
+    by_channel = params.transpose(1, 0, 2).reshape(8, inner)
+    grad_cv = by_channel[:4]
+    grad_cvb = by_channel[4]
+    grad_gate_gain = by_channel[5]
+    grad_sk = jnp.sum(by_channel[6].reshape(head_count, head_size), 1)
     low_step = jnp.pad(grad_ps, ((0, 0), (0, step_pad))).astype(jnp.bfloat16)
     grad_rows = contract_cols(low_gate, gate_full) + contract_cols(low_value, value_full)
     grad_rows = grad_rows + contract_cols(low_step, step_full)

time: 636 us -> 290 us (0.46)
  local copies, waits for them, and re-layouts: 275 us -> 38.6 us
  matrix products: 137 us -> 45.1 us
  other arithmetic: 85.9 us -> 16.8 us
  Pallas kernels: 93.4 us -> 161 us
  loops' own time: 12.5 us -> 0 us
    dynamic_update_slice x24 -> x0, local copies, waits for them, and re-layouts: 155 us -> none  [block_scan_state(): lax.scan(jax.checkpoint(scan_step), start_state, block_inputs)]
    dot_general x48 -> x2, matrix products: 91.3 us -> 0.63 us  [the longest x1 0.37 us: local(): cum = jnp.einsum('ts,bsh->bth', triangle, rate_blocks, precision=HIGH)]
    pallas_call x0 -> x2, Pallas kernels: none -> 66.9 us  [the longest x1 42.5 us: local(): backward(pre_value, pre_gate, grad_branch, ssm_out, states, jnp.concatena...]
    unnamed x153 -> x96, local copies, waits for them, and re-layouts: 34.6 us -> 10.9 us
    dynamic_slice x20 -> x0, local copies, waits for them, and re-layouts: 20.7 us -> none  [block_scan_state(): lax.scan(jax.checkpoint(scan_step), start_state, block_inputs)]
    another operation x49 -> x0, other arithmetic: 19.6 us -> none
    squeeze x16 -> x0, local copies, waits for them, and re-layouts: 16.1 us -> none  [block_scan_state(): lax.scan(jax.checkpoint(scan_step), start_state, block_inputs)]
    another operation x2 -> x0, loops' own time: 12.5 us -> none  [block_scan_state(): lax.scan(jax.checkpoint(scan_step), start_state, block_inputs)]
  transfers between devices with their start and end apart: 7 -> 7, of which waited for: 2 -> 1; matrix products, arithmetic and copies ran while one was open for 33% -> 28% of each run, Pallas kernels for 15% -> 33%
where the time goes in v2:
time: 290 us; the launch traced here: 285 us
  Pallas kernels  161 us (56%)
  matrix products  45.1 us (16%)
  local copies, waits for them, and re-layouts  38.6 us (13%)
  other arithmetic  16.8 us (6%)
  waiting for transfers between devices  13.9 us (5%)
  starting transfers between devices  7.89 us (3%)
    pallas_call x1, Pallas kernels, scatter_rows(): pl.pallas_call(lambda *refs: scatter_kernel(bits, bc_from, *refs), out_sh...  56.7 us
    pallas_call x1, Pallas kernels, local(): backward(pre_value, pre_gate, grad_branch, ssm_out, states, jnp.concatena...  42.5 us
    pallas_call x1, Pallas kernels, gather_rows(): pl.pallas_call(lambda *refs: gather_kernel(bits, *refs), out_shape=jax.Sh...  37.4 us
    pallas_call x1, Pallas kernels, local(): forward(pre_value, pre_gate, grad_branch, *common)  24.4 us
    dot_general x5, matrix products, contract_cols(): lax.dot_general(left, right, (((1,), (1,)), ((), ())), preferred_element_...  15.5 us
    ppermute x7, waiting for transfers between devices, swap(): return lax.ppermute(values, 'tensor', [(0, 1), (1, 0)])  13.9 us
    unnamed x96, local copies, waits for them, and re-layouts  10.9 us
    dot_general x5, matrix products, contract_rows(): lax.dot_general(left, right, (((0,), (0,)), ((), ())), preferred_element_...  10.8 us
  transfers between devices with their start and end apart: 7, of which 1 were waited for; matrix products, arithmetic and copies ran while one was open for 28% of the time, Pallas kernels for 33%

profile of v2, /device:TPU:0, one launch (start us, length us, event | category | flops | bytes accessed | tf_op | source)
XLA Modules:
  0.0 285.1 jit_solution(3115437693821993139)
XLA Ops:
  0.7 3.0 %collective-permute-start.1 = (bf16[24,256]{1,0:T(8,128)(2,1)}, bf16[24,256]{1,0:T(8,128)(2,1)S(1)}, u32[]{:S(2)}, u32[]{:S(2)}) collective-permute-start(bf16[24,256]{1,0:T(8,128)(2,1)} %param.22), channel_id=1, source_target_pairs={{0,1},{1,0},{2,3},{3,2},{4,5},{5,4},{6,7},{7,6},{8,9},{9,8},{10,11... | collective-permute-start | bytes 36872 | tf_op jit(solution)/shard_map/ppermute | solution.py:258
  6.7 2.0 collective-permute-start.2
  16.3 37.4 %gather_rows.1 = bf16[16,48,2688]{2,1,0:T(8,128)(2,1)} custom-call(bf16[48,2688]{1,0:T(8,128)(2,1)} %copy-done.12), custom_call_target="tpu_custom_call" | custom-call | tf_op jit(solution)/shard_map/gather_rows/pallas_call | solution.py:100
  56.0 2.3 fusion.30
  58.3 4.4 %fusion.23.refs_0_ = f32[1024,768]{1,0:T(8,128)} fusion(bf16[768,2688]{1,0:T(8,128)(2,1)} %bitcast.110, bf16[512,768]{1,0:T(8,128)(2,1)S(1)} %copy-done.30, bf16[512,768]{1,0:T(8,128)(2,1)S(1)} %fusion.2, pred[]{:T(512)S(6)} %eq.72), kind=kOutput, calls=%fused_computation.56 | convolution fusion | flops 1215037440 | bytes 5898241 | tf_op jit(solution)/shard_map/dot_general | solution.py:651
  62.9 2.4 copy.99
  66.0 1.9 fusion.12
  67.9 4.3 %fusion.19.refs_1_ = f32[1024,768]{1,0:T(8,128)} fusion(bf16[768,2688]{1,0:T(8,128)(2,1)} %bitcast.111, bf16[512,768]{1,0:T(8,128)(2,1)S(1)} %copy-done.31, bf16[512,768]{1,0:T(8,128)(2,1)S(1)} %fusion.2, pred[]{:T(512)S(6)} %eq.72), kind=kOutput, calls=%fused_computation.52 | convolution fusion | flops 1215037440 | bytes 5898241 | tf_op jit(solution)/shard_map/dot_general | solution.py:650
  72.2 5.3 %fusion.15.refs_2_ = f32[1024,768]{1,0:T(8,128)} fusion(bf16[768,2688]{1,0:T(8,128)(2,1)} %bitcast.112, bf16[512,768]{1,0:T(8,128)(2,1)} %collective-permute-done.2, bf16[512,768]{1,0:T(8,128)(2,1)} %param.33, pred[]{:T(512)S(6)} %eq.72), kind=kOutput, calls=%fused_computation.48 | convolution fusion | flops 1215037440 | bytes 5898241 | tf_op jit(solution)/shard_map/dot_general | solution.py:654
  77.6 24.4 %mixer_forward.1 = (f32[1024,768]{1,0:T(8,128)}, f32[1024,768]{1,0:T(8,128)}, f32[6,4,128,128]{3,2,1,0:T(8,128)}, f32[1024,2]{1,0:T(8,128)}) custom-call(f32[1024,768]{1,0:T(8,128)} %fusion.23.refs_0_, f32[1024,768]{1,0:T(8,128)} %fusion.19.refs_1_, f32[1024,768]{1,0:T(8,128)} %fusion.15.refs_2_, f32[1024,256]{1,0:T(8,128)} %get-tuple-element.133.refs_3_.refs_6_, ...), custom_call_target="tpu_custom_call" | custom-call | tf_op jit(solution)/shard_map/mixer_forward/pallas_call | solution.py:701
  102.6 13.9 %collective-permute-done.3 = f32[2,1024]{0,1:T(8,128)S(1)} collective-permute-done((f32[2,1024]{0,1:T(8,128)}, f32[2,1024]{0,1:T(8,128)S(1)}, u32[]{:S(2)}, u32[]{:S(2)}) %collective-permute-start.3) | collective-permute-done | bytes 8224 | tf_op jit(solution)/shard_map/ppermute | solution.py:258
  119.0 42.5 %mixer_backward.1 = (bf16[1024,768]{1,0:T(8,128)(2,1)}, bf16[1024,768]{1,0:T(8,128)(2,1)}, f32[1024,256]{1,0:T(8,128)}, f32[6,1024,4]{2,1,0:T(8,128)}, f32[6,8,128]{2,1,0:T(8,128)}) custom-call(f32[1024,768]{1,0:T(8,128)} %fusion.23.refs_0_, f32[1024,768]{1,0:T(8,128)} %fusion.19.refs_1_, f32[1024,768]{1,0:T(8,128)} %fusion.15.refs_2_, ...), custom_call_target="tpu_custom_call" | custom-call | tf_op jit(solution)/shard_map/mixer_backward/pallas_call | solution.py:709
  161.5 2.3 multiply_reduce_fusion.3
  167.4 3.2 %fusion.17 = f32[1024,768]{1,0:T(8,128)} fusion(bf16[1024,768]{1,0:T(8,128)(2,1)S(1)} %copy-done.26, bf16[768,2688]{1,0:T(8,128)(2,1)S(1)} %bitcast.116), kind=kOutput, calls=%fused_computation.50 | convolution fusion | flops 1207959552 | bytes 5898240 | tf_op jit(solution)/shard_map/dot_general | solution.py:38
  170.6 3.1 %fusion.21 = f32[1024,768]{1,0:T(8,128)} fusion(bf16[1024,768]{1,0:T(8,128)(2,1)S(1)} %copy-done.27, bf16[768,2688]{1,0:T(8,128)(2,1)S(1)} %bitcast.117), kind=kOutput, calls=%fused_computation.54 | convolution fusion | flops 1207959552 | bytes 5898240 | tf_op jit(solution)/shard_map/dot_general | solution.py:38
  173.7 2.7 slice_bitcast_fusion.1
  176.5 2.6 copy.111
  180.9 3.7 %add_add_fusion = f32[1024,768]{1,0:T(8,128)S(1)} fusion(f32[1024,768]{1,0:T(8,128)} %fusion.17, f32[1024,768]{1,0:T(8,128)} %fusion.21, bf16[1024,12]{0,1:T(8,128)(2,1)S(1)} %get-tuple-element.132, bf16[768,2688]{1,0:T(8,128)(2,1)} %bitcast.113), kind=kOutput, calls=%fused_computation.8 | convolution fusion | flops 202899456 | bytes 9658368 | tf_op jit(solution)/shard_map/dot_general | solution.py:38
  186.5 2.9 fusion.13
  194.9 3.8 %convolution_convert_fusion.1 = bf16[768,768]{1,0:T(8,128)(2,1)S(1)} fusion(bf16[1024,768]{1,0:T(8,128)(2,1)} %get-tuple-element.32, bf16[512,768]{1,0:T(8,128)(2,1)} %copy-done.29, bf16[512,768]{1,0:T(8,128)(2,1)} %copy-done.8, pred[]{:T(512)S(6)} %eq.72), kind=kOutput, calls=%fused_computation.27 | convolution fusion | flops 1215627264 | bytes 4325377 | tf_op jit(solution)/shard_map/dot_general | solution.py:32
  199.8 3.5 %convolution_convert_fusion = bf16[768,768]{1,0:T(8,128)(2,1)S(1)} fusion(bf16[512,768]{1,0:T(8,128)(2,1)} %collective-permute-done.2, bf16[512,768]{1,0:T(8,128)(2,1)} %param.33, pred[]{:T(512)S(6)} %eq.72, f32[1024,768]{1,0:T(8,128)S(1)} %copy-done.7, f32[768]{0:T(1024)S(1)} %copy-done.19, f32[1024]{0:T(1024)S(1)} %get-tuple-element.144), kind=kOutput, calls=%fused_computation.26 | convolution fusion | flops 1217986560 | bytes 5905409 | tf_op jit(solution)/shard_map/dot_general | solution.py:32
  209.3 2.7 fusion.9
  213.3 56.7 %scatter_rows.1 = (f32[48,2688]{1,0:T(8,128)}, f32[24,256]{1,0:T(8,128)}, f32[16,768]{1,0:T(8,128)}) custom-call(bf16[16,48,2688]{2,1,0:T(8,128)(2,1)} %constant_dynamic-update-slice_fusion.4.refs_0_, f32[16,768]{1,0:T(8,128)} %concatenate.92.refs_1_), custom_call_target="tpu_custom_call" | custom-call | tf_op jit(solution)/shard_map/scatter_rows/pallas_call | solution.py:228
  280.0 4.0 %fusion.6 = (f32[512,768]{1,0:T(8,128)}, bf16[512,768]{1,0:T(8,128)(2,1)}) fusion(bf16[512,768]{1,0:T(8,128)(2,1)S(1)} %copy-done.1, bf16[512,768]{1,0:T(8,128)(2,1)} %param.33, f32[512,768]{1,0:T(8,128)S(1)} %get-tuple-element.170, f32[512]{0:T(512)S(1)} %get-tuple-element.121, f32[512]{0:T(512)S(1)} %get-tuple-element.167, f32[768]{0:T(1024)S(1)} %copy-done.16, ...), kind=kLoop, calls=%fused_computation.16 | loop fusion | flops 5111808 | bytes 7873540 | tf_op jit(solution)/shard_map/sub | solution.py:740
  (191 shorter events, 48.3 us)
Async XLA Ops:
  0.6 8.0 %copy-start.11 = (s32[1,1024]{1,0:T(1,128)S(1)}, s32[1,1024]{1,0:T(1,128)}, u32[]{:S(2)}) copy-start(s32[1,1024]{1,0:T(1,128)} %refs_11_.1) | copy-start | bytes 12292
  0.7 9.6 %copy-start.13 = (bf16[48,768]{1,0:T(8,128)(2,1)S(1)}, bf16[48,768]{1,0:T(8,128)(2,1)}, u32[]{:S(2)}) copy-start(bf16[48,768]{1,0:T(8,128)(2,1)} %param.21) | copy-start | bytes 221188
  0.7 9.7 %copy-start.22 = (f32[4,256]{1,0:T(4,128)S(1)}, f32[4,256]{1,0:T(4,128)}, u32[]{:S(2)}) copy-start(f32[4,256]{1,0:T(4,128)} %param.25) | copy-start | bytes 12292
  0.7 10.3 %copy-start.14 = (bf16[48,768]{1,0:T(8,128)(2,1)S(1)}, bf16[48,768]{1,0:T(8,128)(2,1)}, u32[]{:S(2)}) copy-start(bf16[48,768]{1,0:T(8,128)(2,1)} %param.20) | copy-start | bytes 221188
  0.7 10.3 %copy-start.15 = (bf16[48,768]{1,0:T(8,128)(2,1)S(1)}, bf16[48,768]{1,0:T(8,128)(2,1)}, u32[]{:S(2)}) copy-start(bf16[48,768]{1,0:T(8,128)(2,1)} %param.32) | copy-start | bytes 221188
  0.7 10.3 %copy-start.35 = (f32[12]{0:T(128)S(1)}, f32[12]{0:T(128)}, u32[]{:S(2)}) copy-start(f32[12]{0:T(128)} %param.29) | copy-start | bytes 148
  0.7 10.4 %copy-start.23 = (bf16[48,12]{0,1:T(8,128)(2,1)S(1)}, bf16[48,12]{0,1:T(8,128)(2,1)}, u32[]{:S(2)}) copy-start(bf16[48,12]{0,1:T(8,128)(2,1)} %param.23) | copy-start | bytes 3460
  0.7 14.8 %collective-permute-start.1 = (bf16[24,256]{1,0:T(8,128)(2,1)}, bf16[24,256]{1,0:T(8,128)(2,1)S(1)}, u32[]{:S(2)}, u32[]{:S(2)}) collective-permute-start(bf16[24,256]{1,0:T(8,128)(2,1)} %param.22), channel_id=1, source_target_pairs={{0,1},{1,0},{2,3},{3,2},{4,5},{5,4},{6,7},{7,6},{8,9},{9,8},{10,11... | collective-permute-start | bytes 36872 | tf_op jit(solution)/shard_map/ppermute | solution.py:258
  5.1 8.5 %copy-start.21 = (f32[768]{0:T(1024)S(1)}, f32[768]{0:T(1024)}, u32[]{:S(2)}) copy-start(f32[768]{0:T(1024)} %param.26) | copy-start | bytes 9220
  5.1 9.1 %copy-start.25 = (f32[12]{0:T(128)S(1)}, f32[12]{0:T(128)}, u32[]{:S(2)}) copy-start(f32[12]{0:T(128)} %param.30) | copy-start | bytes 148
  5.1 9.8 %copy-start.19 = (f32[768]{0:T(1024)S(1)}, f32[768]{0:T(1024)}, u32[]{:S(2)}) copy-start(f32[768]{0:T(1024)} %param.31) | copy-start | bytes 9220
  5.1 10.4 %copy-start.20 = (bf16[24,256]{1,0:T(8,128)(2,1)S(1)}, bf16[24,256]{1,0:T(8,128)(2,1)}, u32[]{:S(2)}) copy-start(bf16[24,256]{1,0:T(8,128)(2,1)} %param.22) | copy-start | bytes 36868
  6.5 61.4 %copy-start.8 = (bf16[512,768]{1,0:T(8,128)(2,1)}, bf16[512,768]{1,0:T(8,128)(2,1)S(1)}, u32[]{:S(2)}) copy-start(bf16[512,768]{1,0:T(8,128)(2,1)S(1)} %fusion.2) | copy-start | bytes 2359300
  6.6 47.1 %collective-permute-start = (bf16[512,768]{1,0:T(8,128)(2,1)S(1)}, bf16[512,768]{1,0:T(8,128)(2,1)S(1)}, u32[]{:S(2)}, u32[]{:S(2)}) collective-permute-start(bf16[512,768]{1,0:T(8,128)(2,1)S(1)} %fusion.2), channel_id=1, source_target_pairs={{0,1},{1,0},{2,3},{3,2},{4,5},{5,4},{6,7},{7,6},{8,9},{9,8},{10,11... | collective-permute-start | bytes 2359304 | tf_op jit(solution)/shard_map/ppermute | solution.py:258
  6.7 65.6 %collective-permute-start.2 = (bf16[512,768]{1,0:T(8,128)(2,1)}, bf16[512,768]{1,0:T(8,128)(2,1)}, u32[]{:S(2)}, u32[]{:S(2)}) collective-permute-start(bf16[512,768]{1,0:T(8,128)(2,1)} %param.33), channel_id=1, source_target_pairs={{0,1},{1,0},{2,3},{3,2},{4,5},{5,4},{6,7},{7,6},{8,9},{9,8},{10,11... | collective-permute-start | bytes 2359304 | tf_op jit(solution)/shard_map/ppermute | solution.py:258
  16.3 37.4 %copy-start.34 = (f32[12]{0:T(128)S(1)}, f32[12]{0:T(128)}, u32[]{:S(2)}) copy-start(f32[12]{0:T(128)} %param.28) | copy-start | bytes 148
  102.0 14.5 %collective-permute-start.3 = (f32[2,1024]{0,1:T(8,128)}, f32[2,1024]{0,1:T(8,128)S(1)}, u32[]{:S(2)}, u32[]{:S(2)}) collective-permute-start(f32[2,1024]{0,1:T(8,128)} %bitcast.124), channel_id=1, source_target_pairs={{0,1},{1,0},{2,3},{3,2},{4,5},{5,4},{6,7},{7,6},{8,9},{9,8},{10,11... | collective-permute-start | bytes 24584 | tf_op jit(solution)/shard_map/ppermute | solution.py:258
  164.6 6.0 %copy-start.5 = (f32[1024,256]{1,0:T(8,128)}, f32[1024,256]{1,0:T(8,128)S(1)}, u32[]{:S(2)}) copy-start(f32[1024,256]{1,0:T(8,128)S(1)} %pad_add_fusion) | copy-start | bytes 3145732
  165.4 40.5 %collective-permute-start.6 = (bf16[512,256]{1,0:T(8,128)(2,1)}, bf16[512,256]{1,0:T(8,128)(2,1)}, u32[]{:S(2)}, u32[]{:S(2)}) collective-permute-start(bf16[512,256]{1,0:T(8,128)(2,1)} %dynamic-slice_convert_fusion.2), channel_id=1, source_target_pairs={{0,1},{1,0},{2,3},{3,2},{4,5},{5,4},{6,7},{7,6},{8,9},{9,8},{10,11... | collective-permute-start | bytes 786440 | tf_op jit(solution)/shard_map/ppermute | solution.py:258
  180.9 5.6 %copy-start.7 = (f32[1024,768]{1,0:T(8,128)S(1)}, f32[1024,768]{1,0:T(8,128)}, u32[]{:S(2)}) copy-start(f32[1024,768]{1,0:T(8,128)} %get-tuple-element.28) | copy-start | bytes 9437188
  185.6 23.7 %collective-permute-start.5 = (bf16[512,768]{1,0:T(8,128)(2,1)}, bf16[512,768]{1,0:T(8,128)(2,1)}, u32[]{:S(2)}, u32[]{:S(2)}) collective-permute-start(bf16[512,768]{1,0:T(8,128)(2,1)} %dynamic-slice_convert_fusion), channel_id=1, source_target_pairs={{0,1},{1,0},{2,3},{3,2},{4,5},{5,4},{6,7},{7,6},{8,9},{9,8},{10,11... | collective-permute-start | bytes 2359304 | tf_op jit(solution)/shard_map/ppermute | solution.py:258
  186.5 5.0 %copy-start.28 = (bf16[1024,768]{1,0:T(8,128)(2,1)S(1)}, bf16[1024,768]{1,0:T(8,128)(2,1)}, u32[]{:S(2)}) copy-start(bf16[1024,768]{1,0:T(8,128)(2,1)} %get-tuple-element.33) | copy-start | bytes 4718596
  189.4 4.1 %copy-start.2 = (f32[1024,768]{1,0:T(8,128)}, f32[1024,768]{1,0:T(8,128)S(1)}, u32[]{:S(2)}) copy-start(f32[1024,768]{1,0:T(8,128)S(1)} %fusion.13) | copy-start | bytes 9437188
  190.4 89.7 %collective-permute-start.4 = (bf16[512,768]{1,0:T(8,128)(2,1)}, bf16[512,768]{1,0:T(8,128)(2,1)}, u32[]{:S(2)}, u32[]{:S(2)}) collective-permute-start(bf16[512,768]{1,0:T(8,128)(2,1)} %dynamic-slice_convert_fusion.1), channel_id=1, source_target_pairs={{0,1},{1,0},{2,3},{3,2},{4,5},{5,4},{6,7},{7,6},{8,9},{9,8},{10,11... | collective-permute-start | bytes 2359304 | tf_op jit(solution)/shard_map/ppermute | solution.py:258
  (19 other events, 45.0 us)
